TPU v7x, 128 devices: a whole 4x4x4 slice. The times are simulated.
128 devices in a mesh: row: 8 (over x, core), col: 16 (over y, z).
Axes of the slice: x: 4, y: 4, z: 4, core: 2. Of those that a mesh axis runs over, the one named last changes fastest.
Arguments:
- panel: float32 [8192, 512], P(('row', 'col')), as said below
- trailing: float32 [8192, 32768], P('row', 'col'), may hold values from -6 to 6
Outputs:
- r_factor: float32 [512, 512], replicated
- coupling: float32 [512, 32768], P(None, 'col')
- trailing_out: float32 [8192, 32768], P('row', 'col')
Inputs may be any that keep to these rules, and one draw needn't show every extreme that they name: The panel has full column rank with moderate conditioning; its rows carry scales that differ, and its columns share a common component.
All inputs are finite; a program needn't handle non-finite values.
Results may differ from a plain program's by a relative error of at most 0.000086.
Values sent between devices are 32-bit elements; how exact they have to be, the bound alone decides.
No kernel may reach another device: no remote copies, remote signals or barrier semaphores. Data moves between devices by JAX's collectives and lax.ppermute only.
A program may use at most 128 MiB of HBM per device.

v0:
```python
import functools

import jax
import jax.numpy as jnp
from jax import lax
from jax.experimental import pallas as pl
from jax.experimental.pallas import tpu as pltpu
from jax.sharding import PartitionSpec as P

HIGHEST = lax.Precision.HIGHEST
BF16 = jnp.bfloat16
F32 = jnp.float32
GROUP = 32
TILE = 512


def near(i):
    return i ^ 1


def far(i):
    return 3 - i


PAIR = (near, far)
CORE = [(r, r ^ 1) for r in range(8)]
ROW = [[(x * 2 + c, PAIR[c ^ step](x) * 2 + c) for x in range(4) for c in (0, 1)] for step in (0, 1)]


def spots(row):
    core, x = row % 2, row // 2
    bits = ((x ^ (x // 2)) & 1, x // 2)
    out = []
    for half in (0, 1):
        owner = half ^ core
        one = jnp.where(owner == 0, bits[0], bits[1])
        two = jnp.where(owner == 0, bits[1], bits[0])
        out += [owner * 4 + (i ^ one) * 2 + (j ^ two) for i in (0, 1) for j in (0, 1)]
    return out


def places(core, col):
    out = []
    for q in (0, 1):
        place = [(col // 4, col % 4)]
        for step in range(4):
            flip = PAIR[(step % 2) ^ q]
            along_z = core == step // 2
            place = place + [(jnp.where(along_z, y, flip(y)), jnp.where(along_z, flip(z), z)) for y, z in place]
        out += [y * 4 + z for y, z in place]
    return out


def tdot(a, b, precision=HIGHEST):
    return lax.dot_general(a, b, (((0,), (0,)), ((), ())), precision=precision, preferred_element_type=F32)


def spread(v, s):
    return jnp.broadcast_to(v[s:s + 1, :], (8, 128))


def eliminate(slab, off, g):
    nt = g // 8
    width = slab.shape[1] // 128
    sub = lax.broadcasted_iota(jnp.int32, (8, 128), 0)
    rows = [[slab[8 * t:8 * t + 8, 128 * w:128 * w + 128] for w in range(width)] for t in range(nt)]
    cols = [
        [jnp.broadcast_to(rows[t][0][:, off + k:off + k + 1], (8, 128)) if t >= k // 8 else None for t in range(nt)]
        for k in range(g)
    ]
    scale = [None] * nt
    for j in range(g):
        tj, sj = divmod(j, 8)
        d = spread(cols[j][tj], sj)
        inv = 1.0 / d
        root = lax.rsqrt(d)
        scale[tj] = root if sj == 0 else jnp.where(sub >= sj, root, scale[tj])
        f = [None if t < tj else cols[j][t] * inv for t in range(nt)]
        for k in range(j + 1, g):
            a = spread(cols[j][k // 8], k % 8)
            for t in range(k // 8, nt):
                cols[k][t] = cols[k][t] - f[t] * a
        f[tj] = jnp.where(sub > sj, f[tj], 0.0)
        for w in range(width):
            p = spread(rows[tj][w], sj)
            for t in range(tj, nt):
                if t > tj or sj < 7:
                    rows[t][w] = rows[t][w] - f[t] * p
    return jnp.concatenate(
        [jnp.concatenate([rows[t][w] * scale[t] for w in range(width)], axis=1) for t in range(nt)], axis=0
    )


def params(mib):
    return pltpu.CompilerParams(vmem_limit_bytes=mib << 20)


def cheap(times=1):
    return pl.CostEstimate(flops=times * 3 * 10 ** 8, bytes_accessed=times * 10 ** 6, transcendentals=0)


def whole(n=1):
    return [pl.BlockSpec(memory_space=pltpu.VMEM)] * n


FAR = pl.BlockSpec(memory_space=pltpu.HBM)


def split(a):
    high = a.astype(BF16)
    return high, (a - high.astype(F32)).astype(BF16)


def dot(a, b):
    return jnp.dot(a, b, preferred_element_type=F32)


def dot3(a, b):
    return dot(a[0], b[0]) + (dot(a[0], b[1]) + dot(a[1], b[0]))


def factor_kernel(k, nb, *refs):
    earlier, (own, other, w, m) = refs[:k], refs[k:]
    core = lax.axis_index("row") % 2
    first = sum(nb - i for i in range(k))
    for j in range(nb - k):
        half, at = divmod(first + j, own.shape[0] // 128)
        rows = slice(at * 128, at * 128 + 128)
        m[:, j * 128:j * 128 + 128] = jnp.where(core == half, own[rows, :], other[rows, :])
    if k:
        m[:, (nb - k) * 128:nb * 128] = jnp.zeros((128, k * 128), F32)
    ri = lax.broadcasted_iota(jnp.int32, (128, 128), 0)
    ci = lax.broadcasted_iota(jnp.int32, (128, 128), 1)
    m[:, nb * 128:] = jnp.where(ri == ci, 1.0, 0.0)
    for i in range(k):
        at = (k - i) * 128
        known = earlier[i][:, at:]
        width = known.shape[1]
        m[:, :width] = m[:, :width] - tdot(earlier[i][:, at:at + 128], known)
    for q in range(128 // GROUP):
        lo, hi = q * GROUP, (q + 1) * GROUP
        slab = m[lo:hi, :]
        if q:
            slab = slab - tdot(w[0:lo, lo:hi], w[0:lo, :])
        w[lo:hi, :] = eliminate(slab, lo, GROUP)


def factor_rows(k, nb, earlier, packed):
    window = (nb + 1) * 128
    return pl.pallas_call(
        functools.partial(factor_kernel, k, nb),
        out_shape=jax.ShapeDtypeStruct((128, window), F32),
        in_specs=whole(k + 2),
        out_specs=whole()[0],
        scratch_shapes=[pltpu.VMEM((128, window), F32)],
        compiler_params=params(28),
        cost_estimate=cheap(),
        name="factor",
    )(*earlier, *packed)


def gather_pairs(q, step):
    out = []
    for x in range(4):
        for c in (0, 1):
            for y in range(4):
                for z in range(4):
                    flip = PAIR[(step % 2) ^ q]
                    to = (y, flip(z)) if (step // 2) ^ c == 0 else (flip(y), z)
                    out.append(((x * 2 + c) * 16 + y * 4 + z, (x * 2 + c) * 16 + to[0] * 4 + to[1]))
    return out


def gather_panel(panel):
    n = panel.shape[1] // 2
    pieces = [[panel[:, :n]], [panel[:, n:]]]
    for step in range(4):
        held = [p[0] if len(p) == 1 else jnp.concatenate(p, axis=0) for p in pieces]
        pieces = [[h, lax.ppermute(h, ("row", "col"), gather_pairs(q, step))] for q, h in enumerate(held)]
    return pieces[0] + pieces[1]


def turn_kernel(*refs):
    pieces, (o_ref, hi_ref, lo_ref) = refs[:4], refs[4:]
    order = places(lax.axis_index("row") % 2, lax.axis_index("col"))
    for i, ref in enumerate(pieces):
        q = i // 2
        for p in range(8):
            at = pl.multiple_of(order[i * 8 + p] * 64, 64)
            o_ref[pl.ds(at, 64), q * 256:q * 256 + 256] = ref[p * 64:p * 64 + 64, :]
    for j in range(0, 1024, 128):
        hi_ref[:, j:j + 128], lo_ref[:, j:j + 128] = split(jnp.transpose(o_ref[j:j + 128, :]))


def turn(pieces):
    depth, b = pieces[0].shape[0] * 2, pieces[0].shape[1] * 2
    out = jax.ShapeDtypeStruct((b, depth), BF16)
    return pl.pallas_call(
        turn_kernel,
        out_shape=(jax.ShapeDtypeStruct((depth, b), F32), out, out),
        in_specs=whole(4),
        out_specs=whole(3),
        compiler_params=params(28),
        cost_estimate=cheap(10),
        name="turn",
    )(*pieces)


def gram_kernel(p_ref, keep_ref, give_ref, blocks):
    at = 0
    for i in range(4):
        strip = tdot(p_ref[:, i * 128:i * 128 + 128], p_ref[:, i * 128:])
        for j in range(4 - i):
            blocks[at:at + 128, :] = strip[:, j * 128:j * 128 + 128]
            at += 128
    core = lax.axis_index("row") % 2
    keep_ref[...] = blocks[pl.ds(pl.multiple_of(core * 640, 128), 640), :]
    give_ref[...] = blocks[pl.ds(pl.multiple_of((1 - core) * 640, 128), 640), :]


def gram_share(rows):
    half = jax.ShapeDtypeStruct((640, 128), F32)
    return pl.pallas_call(
        gram_kernel,
        out_shape=(half, half),
        in_specs=whole(),
        out_specs=whole(2),
        scratch_shapes=[pltpu.VMEM((1280, 128), F32)],
        compiler_params=params(28),
        cost_estimate=cheap(10),
        name="gram",
    )(rows)


def swap(a, pairs):
    return lax.ppermute(a, "row", pairs)


def columns(first, i):
    return pl.ds(pl.multiple_of(first + i * TILE, TILE), TILE)


def fetch(hbm, buf, sems, first):
    def copy(i):
        return pltpu.make_async_copy(hbm.at[:, columns(first, i)], buf.at[i], sems.at[i])

    for i in range(buf.shape[0]):
        copy(i).start()
    return copy


def share_kernel(first, hi_ref, lo_ref, t_hbm, keep_ref, give_ref, buf, whole_share, sems):
    at_spot = spots(lax.axis_index("row"))
    copy = fetch(t_hbm, buf, sems, first)

    @pl.loop(0, buf.shape[0])
    def _(i):
        copy(i).wait()
        whole_share[...] = dot3((hi_ref[...], lo_ref[...]), split(buf[i]))
        for p in range(8):
            block = pl.ds(pl.multiple_of(at_spot[p] * 64, 64), 64)
            ref = (keep_ref, give_ref)[p // 4]
            ref[p % 4 * 64:p % 4 * 64 + 64, columns(0, i)] = whole_share[block, :]


def share(hi, lo, trailing, first, width):
    depth = trailing.shape[0]
    half = jax.ShapeDtypeStruct((256, width), F32)
    return pl.pallas_call(
        functools.partial(share_kernel, first),
        out_shape=(half, half),
        in_specs=whole(2) + [FAR],
        out_specs=whole(2),
        scratch_shapes=[
            pltpu.VMEM((width // TILE, depth, TILE), F32),
            pltpu.VMEM((512, TILE), F32),
            pltpu.SemaphoreType.DMA((width // TILE,)),
        ],
        compiler_params=params(28),
        cost_estimate=cheap(10),
        name="share",
    )(hi, lo, trailing)


def fold_kernel(k0, k1, g0, g1, keep_ref, give_ref):
    n = k0.shape[1]
    for cols, k, g in ((slice(0, n), k0, g0), (slice(n, 2 * n), k1, g1)):
        give_ref[:, cols] = k[128:, :] + g[128:, :]
        keep_ref[:, cols] = k[:128, :] + g[:128, :]


def fold(keeps, gots):
    out = jax.ShapeDtypeStruct((128, 2 * keeps[0].shape[1]), F32)
    return pl.pallas_call(
        fold_kernel,
        out_shape=(out, out),
        in_specs=whole(4),
        out_specs=whole(2),
        compiler_params=params(28),
        cost_estimate=cheap(),
        name="fold",
    )(*keeps, *gots)


def prepare_kernel(w0, w1, w2, w3, p_ref, r_ref, ihi_ref, ilo_ref, bhi_ref, blo_ref, inv):
    ri = lax.broadcasted_iota(jnp.int32, (128, 128), 0)
    ci = lax.broadcasted_iota(jnp.int32, (128, 128), 1)
    zero = jnp.zeros((128, 128), F32)
    for i, w in enumerate((w0, w1, w2, w3)):
        rows = slice(i * 128, i * 128 + 128)
        for j in range(4):
            cols = slice(j * 128, j * 128 + 128)
            if j < i:
                r_ref[rows, cols] = zero
            else:
                block = w[:, (j - i) * 128:(j - i) * 128 + 128]
                r_ref[rows, cols] = jnp.where(ri <= ci, block, 0.0) if j == i else block
            inv[rows, cols] = w[:, (4 - i + j) * 128:(5 - i + j) * 128] if j <= i else zero
    ihi_ref[...], ilo_ref[...] = split(inv[...])
    turned = split(jnp.transpose(inv[...]))
    for at in range(0, 1024, 256):
        rows = slice(at, at + 256)
        bhi_ref[rows, :], blo_ref[rows, :] = split(dot3(split(p_ref[rows, :]), turned))


def prepare(factors, rows):
    b = rows.shape[1]
    square, tall = (b, b), rows.shape
    return pl.pallas_call(
        prepare_kernel,
        out_shape=[jax.ShapeDtypeStruct(s, t) for s, t in ((square, F32), (square, BF16), (square, BF16), (tall, BF16), (tall, BF16))],
        in_specs=whole(5),
        out_specs=whole(5),
        scratch_shapes=[pltpu.VMEM(square, F32)],
        compiler_params=params(28),
        cost_estimate=cheap(),
        name="prepare",
    )(*factors, rows)


def finish_kernel(first, *refs):
    pieces, (ihi, ilo, bhi, blo, t_hbm) = refs[:4], refs[4:9]
    c_hbm, o_hbm, buf, total, cbuf, in_sems, c_sems, o_sems = refs[-8:]
    n = total.shape[0] // 2
    at_spot = spots(lax.axis_index("row"))
    copy = fetch(t_hbm, buf, in_sems, first)
    tall = buf.shape[1] // 2

    def c_copy(i):
        return pltpu.make_async_copy(cbuf.at[i], c_hbm.at[:, columns(first, i)], c_sems.at[i])

    def o_copy(i, r):
        rows = pl.ds(pl.multiple_of(r * tall, tall), tall)
        return pltpu.make_async_copy(buf.at[i, rows, :], o_hbm.at[rows, columns(first, i)], o_sems.at[2 * i + r])

    @pl.loop(0, buf.shape[0])
    def _(i):
        for p in range(8):
            at = pl.multiple_of(at_spot[p] * 64, 64)
            total[pl.ds(at, 64), :] = pieces[p // 2][p % 2 * 64:p % 2 * 64 + 64, columns(0, i)]
        high, low = split(total[...])
        for rows, depth in ((slice(0, n), n), (slice(n, 2 * n), 2 * n)):
            cbuf[i, rows, :] = dot3((ihi[rows, :depth], ilo[rows, :depth]), (high[:depth, :], low[:depth, :]))
        c_copy(i).start()
        c = split(cbuf[i])
        copy(i).wait()

        @pl.loop(0, 2)
        def _(r):
            rows = pl.ds(pl.multiple_of(r * tall, tall), tall)
            buf[i, rows, :] = buf[i, rows, :] - dot3((bhi[rows, :], blo[rows, :]), c)
            o_copy(i, r).start()

    @pl.loop(0, buf.shape[0])
    def _(i):
        c_copy(i).wait()
        o_copy(i, 0).wait()
        o_copy(i, 1).wait()


def finish(pieces, ihi, ilo, bhi, blo, trailing, first, done):
    depth, width = trailing.shape
    b = ihi.shape[0]
    tiles = pieces[0].shape[1] // TILE
    return pl.pallas_call(
        functools.partial(finish_kernel, first),
        out_shape=(jax.ShapeDtypeStruct((b, width), F32), jax.ShapeDtypeStruct((depth, width), F32)),
        in_specs=whole(8) + [FAR] * (1 + len(done)),
        out_specs=(FAR, FAR),
        scratch_shapes=[
            pltpu.VMEM((tiles, depth, TILE), F32),
            pltpu.VMEM((b, TILE), F32),
            pltpu.VMEM((tiles, b, TILE), F32),
            pltpu.SemaphoreType.DMA((tiles,)),
            pltpu.SemaphoreType.DMA((tiles,)),
            pltpu.SemaphoreType.DMA((2 * tiles,)),
        ],
        input_output_aliases={9 + i: i for i in range(len(done))},
        compiler_params=params(28),
        cost_estimate=cheap(),
        name="finish",
    )(*pieces, ihi, ilo, bhi, blo, trailing, *done)


def after(value, *others):
    return lax.optimization_barrier((value, others))[0]


def local(panel, trailing):
    rows, hi, lo = turn(gather_panel(panel))
    width = trailing.shape[1] // 2
    gram_keep, gram_give = gram_share(rows)
    gram_came = swap(gram_give, CORE)
    gram = gram_keep + gram_came
    came = swap(gram, ROW[0])
    first = share(after(hi, gram), lo, trailing, 0, width)
    gram = after(gram, first[0]) + came
    came = swap(gram, ROW[1])
    second = share(after(hi, gram, first[0]), lo, trailing, width, width)
    gram = gram + came
    second, gram = lax.optimization_barrier((second, gram))
    keep, give = fold((first[0], second[0]), [swap(g, CORE) for g in (first[1], second[1])])

    x_came = swap(give, ROW[0])
    packed = (gram, swap(gram, CORE))
    factors = [factor_rows(0, 4, [], packed)]
    factors.append(factor_rows(1, 4, factors, packed))
    keep, came, factors = lax.optimization_barrier((keep, x_came, factors))
    give, keep = keep[64:] + came[64:], keep[:64] + came[:64]
    came = swap(give, ROW[1])
    factors.append(factor_rows(2, 4, factors, packed))
    factors.append(factor_rows(3, 4, factors, packed))
    own, factors = lax.optimization_barrier((keep + came, factors))
    came = swap(own, ROW[1])
    r_factor, ihi, ilo, bhi, blo = prepare(factors, rows)
    own, came, ihi = lax.optimization_barrier((own, came, ihi))
    done = ()
    own = [jnp.concatenate([own[:, at:at + width], came[:, at:at + width]], axis=0) for at in (0, width)]
    came = [swap(own[0], ROW[0])]
    own[1] = after(own[1], came[0])
    came.append(swap(own[1], ROW[0]))
    own_across = [swap(p, CORE) for p in own]
    for c in (0, 1):
        pieces = [own[c], came[c], own_across[c], swap(came[c], CORE)]
        done = finish(pieces, ihi, ilo, bhi, blo, trailing, c * width, done)
        if c == 0:
            done, came = lax.optimization_barrier((done, came))
    return (r_factor, *done)


def solution(mesh):
    placed = (P(("row", "col"), None), P("row", "col"))
    return jax.shard_map(
        local,
        mesh=mesh,
        in_specs=placed,
        out_specs=(P(), P(None, "col"), P("row", "col")),
        check_vma=False,
    )
```

profile of v0, /device:TPU:1, one launch (start us, length us, event | category | flops | bytes accessed | tf_op | source)
XLA Modules:
  0.0 124.9 jit_solution(10177303774689218234)
XLA Ops:
  0.6 0.9 fusion.2
  1.5 2.2 %collective-permute-start = (f32[64,256]{1,0:T(8,128)S(1)}, f32[64,256]{1,0:T(8,128)S(1)}, u32[]{:S(2)}, u32[]{:S(2)}) collective-permute-start(f32[64,256]{1,0:T(8,128)S(1)} %get-tuple-element.92), channel_id=1, source_target_pairs={{0,1},{1,0},{2,3},{3,2},{4,5},{5,4},{6,7},{7,6},{8,9},{9,8},{10,11... | collective-permute-start | bytes 196616 | tf_op jit(solution)/shard_map/ppermute | solution.py:179
  3.7 1.9 %collective-permute-start.4 = (f32[64,256]{1,0:T(8,128)S(1)}, f32[64,256]{1,0:T(8,128)S(1)}, u32[]{:S(2)}, u32[]{:S(2)}) collective-permute-start(f32[64,256]{1,0:T(8,128)S(1)} %get-tuple-element.91), channel_id=1, source_target_pairs={{0,3},{1,2},{2,1},{3,0},{4,7},{5,6},{6,5},{7,4},{8,11},{9,10},{10,... | collective-permute-start | bytes 196616 | tf_op jit(solution)/shard_map/ppermute | solution.py:179
  5.6 2.7 %collective-permute-start.1 = (f32[128,256]{1,0:T(8,128)S(1)}, f32[128,256]{1,0:T(8,128)S(1)}, u32[]{:S(2)}, u32[]{:S(2)}) collective-permute-start(f32[128,256]{1,0:T(8,128)S(1)} %pad_maximum_fusion.6), channel_id=1, source_target_pairs={{0,3},{1,2},{2,1},{3,0},{4,7},{5,6},{6,5},{7,4},{8,11},{9,10},{10,... | collective-permute-start | bytes 393224 | tf_op jit(solution)/shard_map/ppermute | solution.py:179
  8.4 0.1 collective-permute-start.5
  8.5 2.3 %collective-permute-done.1 = f32[128,256]{1,0:T(8,128)S(1)} collective-permute-done((f32[128,256]{1,0:T(8,128)S(1)}, f32[128,256]{1,0:T(8,128)S(1)}, u32[]{:S(2)}, u32[]{:S(2)}) %collective-permute-start.1) | collective-permute-done | bytes 131104 | tf_op jit(solution)/shard_map/ppermute | solution.py:179
  10.8 1.7 %collective-permute-start.2 = (f32[256,256]{1,0:T(8,128)S(1)}, f32[256,256]{1,0:T(8,128)S(1)}, u32[]{:S(2)}, u32[]{:S(2)}) collective-permute-start(f32[256,256]{1,0:T(8,128)S(1)} %pad_maximum_fusion.4), channel_id=1, source_target_pairs={{0,4},{1,5},{2,6},{3,7},{4,0},{5,1},{6,2},{7,3},{8,12},{9,13},{10,... | collective-permute-start | bytes 786440 | tf_op jit(solution)/shard_map/ppermute | solution.py:179
  12.5 3.9 %collective-permute-start.6 = (f32[256,256]{1,0:T(8,128)S(1)}, f32[256,256]{1,0:T(8,128)S(1)}, u32[]{:S(2)}, u32[]{:S(2)}) collective-permute-start(f32[256,256]{1,0:T(8,128)S(1)} %pad_maximum_fusion.5), channel_id=1, source_target_pairs={{0,12},{1,13},{2,14},{3,15},{4,8},{5,9},{6,10},{7,11},{8,4},{9,5},... | collective-permute-start | bytes 786440 | tf_op jit(solution)/shard_map/ppermute | solution.py:179
  16.4 1.5 %collective-permute-done.2 = f32[256,256]{1,0:T(8,128)S(1)} collective-permute-done((f32[256,256]{1,0:T(8,128)S(1)}, f32[256,256]{1,0:T(8,128)S(1)}, u32[]{:S(2)}, u32[]{:S(2)}) %collective-permute-start.2) | collective-permute-done | bytes 262176 | tf_op jit(solution)/shard_map/ppermute | solution.py:179
  18.0 2.0 %collective-permute-start.3 = (f32[512,256]{1,0:T(8,128)S(1)}, f32[512,256]{1,0:T(8,128)S(1)}, u32[]{:S(2)}, u32[]{:S(2)}) collective-permute-start(f32[512,256]{1,0:T(8,128)S(1)} %pad_maximum_fusion.refs_0_), channel_id=1, source_target_pairs={{0,12},{1,13},{2,14},{3,15},{4,8},{5,9},{6,10},{7,11},{8,4},{9,5},... | collective-permute-start | bytes 1572872 | tf_op jit(solution)/shard_map/ppermute | solution.py:179
  20.0 0.2 collective-permute-done.6
  20.3 7.3 %collective-permute-done.3.refs_1_ = f32[512,256]{1,0:T(8,128)S(1)} collective-permute-done((f32[512,256]{1,0:T(8,128)S(1)}, f32[512,256]{1,0:T(8,128)S(1)}, u32[]{:S(2)}, u32[]{:S(2)}) %collective-permute-start.3) | collective-permute-done | bytes 524320 | tf_op jit(solution)/shard_map/ppermute | solution.py:179
  27.6 1.0 collective-permute-done.7.refs_3_
  28.6 0.9 turn.1
  29.6 3.1 %gram.1 = (f32[640,128]{1,0:T(8,128)S(1)}, f32[640,128]{1,0:T(8,128)S(1)}) custom-call(f32[1024,512]{1,0:T(8,128)S(1)} %get-tuple-element.46.p_ref), custom_call_target="tpu_custom_call" | custom-call | flops 3000000000 | bytes 10000000 | tf_op jit(solution)/shard_map/gram/pallas_call | solution.py:223
  32.7 6.4 %collective-permute-start.8 = (f32[640,128]{1,0:T(8,128)S(1)}, f32[640,128]{1,0:T(8,128)S(1)}, u32[]{:S(2)}, u32[]{:S(2)}) collective-permute-start(f32[640,128]{1,0:T(8,128)S(1)} %get-tuple-element.48), channel_id=1, source_target_pairs={{0,16},{16,0},{32,48},{48,32},{64,80},{80,64},{96,112},{112,96},{1... | collective-permute-start | bytes 983048 | tf_op jit(solution)/shard_map/ppermute | solution.py:236
  39.1 1.3 %collective-permute-done.8 = f32[640,128]{1,0:T(8,128)S(1)} collective-permute-done((f32[640,128]{1,0:T(8,128)S(1)}, f32[640,128]{1,0:T(8,128)S(1)}, u32[]{:S(2)}, u32[]{:S(2)}) %collective-permute-start.8) | collective-permute-done | bytes 327712 | tf_op jit(solution)/shard_map/ppermute | solution.py:236
  40.4 2.6 %collective-permute-start.9 = (f32[640,128]{1,0:T(8,128)S(1)}, f32[640,128]{1,0:T(8,128)S(1)}, u32[]{:S(2)}, u32[]{:S(2)}) collective-permute-start(f32[640,128]{1,0:T(8,128)S(1)} %add.18), channel_id=1, source_target_pairs={{0,32},{16,112},{32,0},{48,80},{64,96},{80,48},{96,64},{112,16},{1... | collective-permute-start | bytes 983048 | tf_op jit(solution)/shard_map/ppermute | solution.py:236
  42.9 4.5 %share.2 = (f32[256,1024]{1,0:T(8,128)S(1)}, f32[256,1024]{1,0:T(8,128)S(1)}) custom-call(bf16[512,1024]{1,0:T(8,128)(2,1)S(1)} %get-tuple-element.53.hi_ref, bf16[512,1024]{1,0:T(8,128)(2,1)S(1)} %get-tuple-element.50.lo_ref, f32[1024,2048]{1,0:T(8,128)S(1)} %bitcast.1), custom_call_target="tpu_custom_call" | custom-call | flops 3000000000 | bytes 10000000 | tf_op jit(solution)/shard_map/share/pallas_call | solution.py:269
  47.5 0.1 collective-permute-done.9
  47.6 0.4 collective-permute-start.10
  48.0 2.8 %collective-permute-start.11 = (f32[256,1024]{1,0:T(8,128)S(1)}, f32[256,1024]{1,0:T(8,128)S(1)}, u32[]{:S(2)}, u32[]{:S(2)}) collective-permute-start(f32[256,1024]{1,0:T(8,128)S(1)} %get-tuple-element.57), channel_id=1, source_target_pairs={{0,16},{16,0},{32,48},{48,32},{64,80},{80,64},{96,112},{112,96},{1... | collective-permute-start | bytes 3145736 | tf_op jit(solution)/shard_map/ppermute | solution.py:236
  50.8 4.5 %share.3 = (f32[256,1024]{1,0:T(8,128)S(1)}, f32[256,1024]{1,0:T(8,128)S(1)}) custom-call(bf16[512,1024]{1,0:T(8,128)(2,1)S(1)} %get-tuple-element.53.hi_ref, bf16[512,1024]{1,0:T(8,128)(2,1)S(1)} %get-tuple-element.50.lo_ref, f32[1024,2048]{1,0:T(8,128)S(1)} %bitcast.1), custom_call_target="tpu_custom_call" | custom-call | flops 3000000000 | bytes 10000000 | tf_op jit(solution)/shard_map/share/pallas_call | solution.py:269
  55.3 1.1 collective-permute-start.12
  56.4 2.3 %collective-permute-done.12.g1 = f32[256,1024]{1,0:T(8,128)S(1)} collective-permute-done((f32[256,1024]{1,0:T(8,128)S(1)}, f32[256,1024]{1,0:T(8,128)S(1)}, u32[]{:S(2)}, u32[]{:S(2)}) %collective-permute-start.12) | collective-permute-done | bytes 1048608 | tf_op jit(solution)/shard_map/ppermute | solution.py:236
  58.7 0.2 fold.1
  58.9 2.6 %collective-permute-start.13 = (f32[128,2048]{1,0:T(8,128)S(1)}, f32[128,2048]{1,0:T(8,128)S(1)}, u32[]{:S(2)}, u32[]{:S(2)}) collective-permute-start(f32[128,2048]{1,0:T(8,128)S(1)} %get-tuple-element.60), channel_id=1, source_target_pairs={{0,32},{16,112},{32,0},{48,80},{64,96},{80,48},{96,64},{112,16},{1... | collective-permute-start | bytes 3145736 | tf_op jit(solution)/shard_map/ppermute | solution.py:236
  61.5 1.6 %collective-permute-done.14.refs_1_.refs_2_.refs_3_.refs_4_ = f32[640,128]{1,0:T(8,128)S(1)} collective-permute-done((f32[640,128]{1,0:T(8,128)S(1)}, f32[640,128]{1,0:T(8,128)S(1)}, u32[]{:S(2)}, u32[]{:S(2)}) %collective-permute-start.14) | collective-permute-done | bytes 327712 | tf_op jit(solution)/shard_map/ppermute | solution.py:236
  63.1 3.6 %factor.4.refs_0_.w0 = f32[128,640]{1,0:T(8,128)S(1)} custom-call(f32[640,128]{1,0:T(8,128)S(1)} %add.20.refs_0_.refs_1_.refs_2_.refs_3_, f32[640,128]{1,0:T(8,128)S(1)} %collective-permute-done.14.refs_1_.refs_2_.refs_3_.refs_4_), custom_call_target="tpu_custom_call" | custom-call | flops 300000000 | bytes 1000000 | tf_op jit(solution)/shard_map/factor/pallas_call | solution.py:150
  66.7 4.0 %factor.5.refs_1_.w1 = f32[128,640]{1,0:T(8,128)S(1)} custom-call(f32[128,640]{1,0:T(8,128)S(1)} %factor.4.refs_0_.w0, f32[640,128]{1,0:T(8,128)S(1)} %add.20.refs_0_.refs_1_.refs_2_.refs_3_, f32[640,128]{1,0:T(8,128)S(1)} %collective-permute-done.14.refs_1_.refs_2_.refs_3_.refs_4_), custom_call_target="tpu_custom_call" | custom-call | flops 300000000 | bytes 1000000 | tf_op jit(solution)/shard_map/factor/pallas_call | solution.py:150
  70.8 3.1 %collective-permute-done.13 = f32[128,2048]{1,0:T(8,128)S(1)} collective-permute-done((f32[128,2048]{1,0:T(8,128)S(1)}, f32[128,2048]{1,0:T(8,128)S(1)}, u32[]{:S(2)}, u32[]{:S(2)}) %collective-permute-start.13) | collective-permute-done | bytes 1048608 | tf_op jit(solution)/shard_map/ppermute | solution.py:236
  74.0 4.1 %factor.6.refs_2_.w2 = f32[128,640]{1,0:T(8,128)S(1)} custom-call(f32[128,640]{1,0:T(8,128)S(1)} %factor.4.refs_0_.w0, f32[128,640]{1,0:T(8,128)S(1)} %factor.5.refs_1_.w1, f32[640,128]{1,0:T(8,128)S(1)} %add.20.refs_0_.refs_1_.refs_2_.refs_3_, f32[640,128]{1,0:T(8,128)S(1)} %collective-permute-done.14.refs_1_.refs_2_.refs_3_.refs_4_), custom_call_target="tpu_custom_call" | custom-call | flops 300000000 | bytes 1000000 | tf_op jit(solution)/shard_map/factor/pallas_call | solution.py:150
  78.1 4.2 %factor.7.w3 = f32[128,640]{1,0:T(8,128)S(1)} custom-call(f32[128,640]{1,0:T(8,128)S(1)} %factor.4.refs_0_.w0, f32[128,640]{1,0:T(8,128)S(1)} %factor.5.refs_1_.w1, f32[128,640]{1,0:T(8,128)S(1)} %factor.6.refs_2_.w2, f32[640,128]{1,0:T(8,128)S(1)} %add.20.refs_0_.refs_1_.refs_2_.refs_3_, f32[640,128]{1,0:T(8,128)S(1)} %collective-permute-done.14.refs_1_.refs_2_.refs_3_.refs_4_), custom_call_target="tpu_custom_call" | custom-call | flops 300000000 | bytes 1000000 | tf_op jit(solution)/shard_map/factor/pallas_call | solution.py:150
  82.4 1.5 %collective-permute-start.16 = (f32[64,2048]{1,0:T(8,128)S(1)}, f32[64,2048]{1,0:T(8,128)S(1)}, u32[]{:S(2)}, u32[]{:S(2)}) collective-permute-start(f32[64,2048]{1,0:T(8,128)S(1)} %add_add_fusion), channel_id=1, source_target_pairs={{0,96},{16,48},{32,64},{48,16},{64,32},{80,112},{96,0},{112,80},{1... | collective-permute-start | bytes 1572872 | tf_op jit(solution)/shard_map/ppermute | solution.py:236
  84.0 3.0 %prepare.1 = (f32[512,512]{1,0:T(8,128)}, bf16[512,512]{1,0:T(8,128)(2,1)S(1)}, bf16[512,512]{1,0:T(8,128)(2,1)S(1)}, bf16[1024,512]{1,0:T(8,128)(2,1)S(1)}, bf16[1024,512]{1,0:T(8,128)(2,1)S(1)}) custom-call(f32[128,640]{1,0:T(8,128)S(1)} %factor.4.refs_0_.w0, f32[128,640]{1,0:T(8,128)S(1)} %factor.5.refs_1_.w1, f32[128,640]{1,0:T(8,128)S(1)} %factor.6.refs_2_.w2, ...), custom_call_target="tpu_custom_call" | custom-call | flops 300000000 | bytes 1000000 | tf_op jit(solution)/shard_map/prepare/pallas_call | solution.py:329
  87.0 3.9 %collective-permute-done.16 = f32[64,2048]{1,0:T(8,128)S(1)} collective-permute-done((f32[64,2048]{1,0:T(8,128)S(1)}, f32[64,2048]{1,0:T(8,128)S(1)}, u32[]{:S(2)}, u32[]{:S(2)}) %collective-permute-start.16) | collective-permute-done | bytes 524320 | tf_op jit(solution)/shard_map/ppermute | solution.py:236
  90.9 0.1 fusion
  91.0 2.6 %collective-permute-start.17 = (f32[128,1024]{1,0:T(8,128)S(1)}, f32[128,1024]{1,0:T(8,128)S(1)}, u32[]{:S(2)}, u32[]{:S(2)}) collective-permute-start(f32[128,1024]{1,0:T(8,128)S(1)} %pad_maximum_fusion.3.refs_0_), channel_id=1, source_target_pairs={{0,32},{16,112},{32,0},{48,80},{64,96},{80,48},{96,64},{112,16},{1... | collective-permute-start | bytes 1572872 | tf_op jit(solution)/shard_map/ppermute | solution.py:236
  93.6 3.2 %collective-permute-start.18 = (f32[128,1024]{1,0:T(8,128)S(1)}, f32[128,1024]{1,0:T(8,128)S(1)}, u32[]{:S(2)}, u32[]{:S(2)}) collective-permute-start(f32[128,1024]{1,0:T(8,128)S(1)} %pad_maximum_fusion.3.refs_0_), channel_id=1, source_target_pairs={{0,16},{16,0},{32,48},{48,32},{64,80},{80,64},{96,112},{112,96},{1... | collective-permute-start | bytes 1572872 | tf_op jit(solution)/shard_map/ppermute | solution.py:236
  96.8 4.1 %collective-permute-done.17.refs_1_ = f32[128,1024]{1,0:T(8,128)S(1)} collective-permute-done((f32[128,1024]{1,0:T(8,128)S(1)}, f32[128,1024]{1,0:T(8,128)S(1)}, u32[]{:S(2)}, u32[]{:S(2)}) %collective-permute-start.17) | collective-permute-done | bytes 524320 | tf_op jit(solution)/shard_map/ppermute | solution.py:236
  100.9 5.0 %collective-permute-start.19 = (f32[128,1024]{1,0:T(8,128)S(1)}, f32[128,1024]{1,0:T(8,128)S(1)}, u32[]{:S(2)}, u32[]{:S(2)}) collective-permute-start(f32[128,1024]{1,0:T(8,128)S(1)} %collective-permute-done.17.refs_1_), channel_id=1, source_target_pairs={{0,16},{16,0},{32,48},{48,32},{64,80},{80,64},{96,112},{112,96},{1... | collective-permute-start | bytes 1572872 | tf_op jit(solution)/shard_map/ppermute | solution.py:236
  106.0 1.3 %collective-permute-start.20 = (f32[128,1024]{1,0:T(8,128)S(1)}, f32[128,1024]{1,0:T(8,128)S(1)}, u32[]{:S(2)}, u32[]{:S(2)}) collective-permute-start(f32[128,1024]{1,0:T(8,128)S(1)} %pad_maximum_fusion.2.refs_0_), channel_id=1, source_target_pairs={{0,32},{16,112},{32,0},{48,80},{64,96},{80,48},{96,64},{112,16},{1... | collective-permute-start | bytes 1572872 | tf_op jit(solution)/shard_map/ppermute | solution.py:236
  107.3 0.2 collective-permute-done.19.refs_3_
  107.4 7.5 %finish.2 = (f32[512,2048]{1,0:T(8,128)}, f32[1024,2048]{1,0:T(8,128)}) custom-call(f32[128,1024]{1,0:T(8,128)S(1)} %pad_maximum_fusion.3.refs_0_, f32[128,1024]{1,0:T(8,128)S(1)} %collective-permute-done.17.refs_1_, f32[128,1024]{1,0:T(8,128)S(1)} %collective-permute-done.18.refs_2_, f32[128,1024]{1,0:T(8,128)S(1)} %collective-permute-done.19.refs_3_, ...), custom_call_target="tpu_custom_call" | custom-call | flops 300000000 | bytes 1000000 | tf_op jit(solution)/shard_map/finish/pallas_call | solution.py:385
  115.0 0.3 collective-permute-done.20.refs_1_
  115.3 0.2 collective-permute-start.22
  115.4 1.8 %collective-permute-done.22.refs_3_ = f32[128,1024]{1,0:T(8,128)S(1)} collective-permute-done((f32[128,1024]{1,0:T(8,128)S(1)}, f32[128,1024]{1,0:T(8,128)S(1)}, u32[]{:S(2)}, u32[]{:S(2)}) %collective-permute-start.22) | collective-permute-done | bytes 524320 | tf_op jit(solution)/shard_map/ppermute | solution.py:236
  117.2 7.5 %finish.3 = (f32[512,2048]{1,0:T(8,128)}, f32[1024,2048]{1,0:T(8,128)}) custom-call(f32[128,1024]{1,0:T(8,128)S(1)} %pad_maximum_fusion.2.refs_0_, f32[128,1024]{1,0:T(8,128)S(1)} %collective-permute-done.20.refs_1_, f32[128,1024]{1,0:T(8,128)S(1)} %collective-permute-done.21.refs_2_, ...), custom_call_target="tpu_custom_call", output_to_operand_aliasing={{0}: (9, {}), {1}: (10, {})} | custom-call | flops 300000000 | bytes 1000000 | tf_op jit(solution)/shard_map/finish/pallas_call | solution.py:385
  (30 shorter events, 0.7 us)
Async XLA Ops:
  1.5 4.1 %collective-permute-start = (f32[64,256]{1,0:T(8,128)S(1)}, f32[64,256]{1,0:T(8,128)S(1)}, u32[]{:S(2)}, u32[]{:S(2)}) collective-permute-start(f32[64,256]{1,0:T(8,128)S(1)} %get-tuple-element.92), channel_id=1, source_target_pairs={{0,1},{1,0},{2,3},{3,2},{4,5},{5,4},{6,7},{7,6},{8,9},{9,8},{10,11... | collective-permute-start | bytes 196616 | tf_op jit(solution)/shard_map/ppermute | solution.py:179
  3.7 4.7 %collective-permute-start.4 = (f32[64,256]{1,0:T(8,128)S(1)}, f32[64,256]{1,0:T(8,128)S(1)}, u32[]{:S(2)}, u32[]{:S(2)}) collective-permute-start(f32[64,256]{1,0:T(8,128)S(1)} %get-tuple-element.91), channel_id=1, source_target_pairs={{0,3},{1,2},{2,1},{3,0},{4,7},{5,6},{6,5},{7,4},{8,11},{9,10},{10,... | collective-permute-start | bytes 196616 | tf_op jit(solution)/shard_map/ppermute | solution.py:179
  5.6 5.1 %collective-permute-start.1 = (f32[128,256]{1,0:T(8,128)S(1)}, f32[128,256]{1,0:T(8,128)S(1)}, u32[]{:S(2)}, u32[]{:S(2)}) collective-permute-start(f32[128,256]{1,0:T(8,128)S(1)} %pad_maximum_fusion.6), channel_id=1, source_target_pairs={{0,3},{1,2},{2,1},{3,0},{4,7},{5,6},{6,5},{7,4},{8,11},{9,10},{10,... | collective-permute-start | bytes 393224 | tf_op jit(solution)/shard_map/ppermute | solution.py:179
  8.4 4.1 %collective-permute-start.5 = (f32[128,256]{1,0:T(8,128)S(1)}, f32[128,256]{1,0:T(8,128)S(1)}, u32[]{:S(2)}, u32[]{:S(2)}) collective-permute-start(f32[128,256]{1,0:T(8,128)S(1)} %pad_maximum_fusion.7), channel_id=1, source_target_pairs={{0,1},{1,0},{2,3},{3,2},{4,5},{5,4},{6,7},{7,6},{8,9},{9,8},{10,11... | collective-permute-start | bytes 393224 | tf_op jit(solution)/shard_map/ppermute | solution.py:179
  10.8 7.2 %collective-permute-start.2 = (f32[256,256]{1,0:T(8,128)S(1)}, f32[256,256]{1,0:T(8,128)S(1)}, u32[]{:S(2)}, u32[]{:S(2)}) collective-permute-start(f32[256,256]{1,0:T(8,128)S(1)} %pad_maximum_fusion.4), channel_id=1, source_target_pairs={{0,4},{1,5},{2,6},{3,7},{4,0},{5,1},{6,2},{7,3},{8,12},{9,13},{10,... | collective-permute-start | bytes 786440 | tf_op jit(solution)/shard_map/ppermute | solution.py:179
  12.5 7.7 %collective-permute-start.6 = (f32[256,256]{1,0:T(8,128)S(1)}, f32[256,256]{1,0:T(8,128)S(1)}, u32[]{:S(2)}, u32[]{:S(2)}) collective-permute-start(f32[256,256]{1,0:T(8,128)S(1)} %pad_maximum_fusion.5), channel_id=1, source_target_pairs={{0,12},{1,13},{2,14},{3,15},{4,8},{5,9},{6,10},{7,11},{8,4},{9,5},... | collective-permute-start | bytes 786440 | tf_op jit(solution)/shard_map/ppermute | solution.py:179
  18.0 9.6 %collective-permute-start.3 = (f32[512,256]{1,0:T(8,128)S(1)}, f32[512,256]{1,0:T(8,128)S(1)}, u32[]{:S(2)}, u32[]{:S(2)}) collective-permute-start(f32[512,256]{1,0:T(8,128)S(1)} %pad_maximum_fusion.refs_0_), channel_id=1, source_target_pairs={{0,12},{1,13},{2,14},{3,15},{4,8},{5,9},{6,10},{7,11},{8,4},{9,5},... | collective-permute-start | bytes 1572872 | tf_op jit(solution)/shard_map/ppermute | solution.py:179
  20.2 8.4 %collective-permute-start.7 = (f32[512,256]{1,0:T(8,128)S(1)}, f32[512,256]{1,0:T(8,128)S(1)}, u32[]{:S(2)}, u32[]{:S(2)}) collective-permute-start(f32[512,256]{1,0:T(8,128)S(1)} %pad_maximum_fusion.1.refs_2_), channel_id=1, source_target_pairs={{0,4},{1,5},{2,6},{3,7},{4,0},{5,1},{6,2},{7,3},{8,12},{9,13},{10,... | collective-permute-start | bytes 1572872 | tf_op jit(solution)/shard_map/ppermute | solution.py:179
  28.6 14.3 %slice-start = ((s8[8388608]{0:T(1024)(128)(4,1)}), s8[4194304]{0:T(1024)(128)(4,1)S(1)}, s32[]{:S(2)}) async-start(s8[8388608]{0:T(1024)(128)(4,1)} %bitcast), calls=%async_computation | async-start | bytes 8388608
  29.6 13.4 %slice-start.1 = ((s8[8388608]{0:T(1024)(128)(4,1)}), s8[4194304]{0:T(1024)(128)(4,1)S(1)}, s32[]{:S(2)}) async-start(s8[8388608]{0:T(1024)(128)(4,1)} %bitcast), calls=%async_computation.1 | async-start | bytes 8388608
  32.7 7.6 %collective-permute-start.8 = (f32[640,128]{1,0:T(8,128)S(1)}, f32[640,128]{1,0:T(8,128)S(1)}, u32[]{:S(2)}, u32[]{:S(2)}) collective-permute-start(f32[640,128]{1,0:T(8,128)S(1)} %get-tuple-element.48), channel_id=1, source_target_pairs={{0,16},{16,0},{32,48},{48,32},{64,80},{80,64},{96,112},{112,96},{1... | collective-permute-start | bytes 983048 | tf_op jit(solution)/shard_map/ppermute | solution.py:236
  40.4 7.2 %collective-permute-start.9 = (f32[640,128]{1,0:T(8,128)S(1)}, f32[640,128]{1,0:T(8,128)S(1)}, u32[]{:S(2)}, u32[]{:S(2)}) collective-permute-start(f32[640,128]{1,0:T(8,128)S(1)} %add.18), channel_id=1, source_target_pairs={{0,32},{16,112},{32,0},{48,80},{64,96},{80,48},{96,64},{112,16},{1... | collective-permute-start | bytes 983048 | tf_op jit(solution)/shard_map/ppermute | solution.py:236
  47.6 7.7 %collective-permute-start.10 = (f32[640,128]{1,0:T(8,128)S(1)}, f32[640,128]{1,0:T(8,128)S(1)}, u32[]{:S(2)}, u32[]{:S(2)}) collective-permute-start(f32[640,128]{1,0:T(8,128)S(1)} %add.19), channel_id=1, source_target_pairs={{0,96},{16,48},{32,64},{48,16},{64,32},{80,112},{96,0},{112,80},{1... | collective-permute-start | bytes 983048 | tf_op jit(solution)/shard_map/ppermute | solution.py:236
  48.0 8.4 %collective-permute-start.11 = (f32[256,1024]{1,0:T(8,128)S(1)}, f32[256,1024]{1,0:T(8,128)S(1)}, u32[]{:S(2)}, u32[]{:S(2)}) collective-permute-start(f32[256,1024]{1,0:T(8,128)S(1)} %get-tuple-element.57), channel_id=1, source_target_pairs={{0,16},{16,0},{32,48},{48,32},{64,80},{80,64},{96,112},{112,96},{1... | collective-permute-start | bytes 3145736 | tf_op jit(solution)/shard_map/ppermute | solution.py:236
  55.3 3.3 %collective-permute-start.12 = (f32[256,1024]{1,0:T(8,128)S(1)}, f32[256,1024]{1,0:T(8,128)S(1)}, u32[]{:S(2)}, u32[]{:S(2)}) collective-permute-start(f32[256,1024]{1,0:T(8,128)S(1)} %get-tuple-element.58), channel_id=1, source_target_pairs={{0,16},{16,0},{32,48},{48,32},{64,80},{80,64},{96,112},{112,96},{1... | collective-permute-start | bytes 3145736 | tf_op jit(solution)/shard_map/ppermute | solution.py:236
  58.9 14.9 %collective-permute-start.13 = (f32[128,2048]{1,0:T(8,128)S(1)}, f32[128,2048]{1,0:T(8,128)S(1)}, u32[]{:S(2)}, u32[]{:S(2)}) collective-permute-start(f32[128,2048]{1,0:T(8,128)S(1)} %get-tuple-element.60), channel_id=1, source_target_pairs={{0,32},{16,112},{32,0},{48,80},{64,96},{80,48},{96,64},{112,16},{1... | collective-permute-start | bytes 3145736 | tf_op jit(solution)/shard_map/ppermute | solution.py:236
  61.5 1.6 %collective-permute-start.14 = (f32[640,128]{1,0:T(8,128)S(1)}, f32[640,128]{1,0:T(8,128)S(1)}, u32[]{:S(2)}, u32[]{:S(2)}) collective-permute-start(f32[640,128]{1,0:T(8,128)S(1)} %add.20.refs_0_.refs_1_.refs_2_.refs_3_), channel_id=1, source_target_pairs={{0,16},{16,0},{32,48},{48,32},{64,80},{80,64},{96,112},{112,96},{1... | collective-permute-start | bytes 983048 | tf_op jit(solution)/shard_map/ppermute | solution.py:236
  73.9 8.4 %collective-permute-start.15 = (f32[64,2048]{1,0:T(8,128)S(1)}, f32[64,2048]{1,0:T(8,128)S(1)}, u32[]{:S(2)}, u32[]{:S(2)}) collective-permute-start(f32[64,2048]{1,0:T(8,128)S(1)} %slice_add_fusion), channel_id=1, source_target_pairs={{0,96},{16,48},{32,64},{48,16},{64,32},{80,112},{96,0},{112,80},{1... | collective-permute-start | bytes 1572872 | tf_op jit(solution)/shard_map/ppermute | solution.py:236
  82.4 8.4 %collective-permute-start.16 = (f32[64,2048]{1,0:T(8,128)S(1)}, f32[64,2048]{1,0:T(8,128)S(1)}, u32[]{:S(2)}, u32[]{:S(2)}) collective-permute-start(f32[64,2048]{1,0:T(8,128)S(1)} %add_add_fusion), channel_id=1, source_target_pairs={{0,96},{16,48},{32,64},{48,16},{64,32},{80,112},{96,0},{112,80},{1... | collective-permute-start | bytes 1572872 | tf_op jit(solution)/shard_map/ppermute | solution.py:236
  91.0 9.9 %collective-permute-start.17 = (f32[128,1024]{1,0:T(8,128)S(1)}, f32[128,1024]{1,0:T(8,128)S(1)}, u32[]{:S(2)}, u32[]{:S(2)}) collective-permute-start(f32[128,1024]{1,0:T(8,128)S(1)} %pad_maximum_fusion.3.refs_0_), channel_id=1, source_target_pairs={{0,32},{16,112},{32,0},{48,80},{64,96},{80,48},{96,64},{112,16},{1... | collective-permute-start | bytes 1572872 | tf_op jit(solution)/shard_map/ppermute | solution.py:236
  93.6 13.7 %collective-permute-start.18 = (f32[128,1024]{1,0:T(8,128)S(1)}, f32[128,1024]{1,0:T(8,128)S(1)}, u32[]{:S(2)}, u32[]{:S(2)}) collective-permute-start(f32[128,1024]{1,0:T(8,128)S(1)} %pad_maximum_fusion.3.refs_0_), channel_id=1, source_target_pairs={{0,16},{16,0},{32,48},{48,32},{64,80},{80,64},{96,112},{112,96},{1... | collective-permute-start | bytes 1572872 | tf_op jit(solution)/shard_map/ppermute | solution.py:236
  100.9 6.5 %collective-permute-start.19 = (f32[128,1024]{1,0:T(8,128)S(1)}, f32[128,1024]{1,0:T(8,128)S(1)}, u32[]{:S(2)}, u32[]{:S(2)}) collective-permute-start(f32[128,1024]{1,0:T(8,128)S(1)} %collective-permute-done.17.refs_1_), channel_id=1, source_target_pairs={{0,16},{16,0},{32,48},{48,32},{64,80},{80,64},{96,112},{112,96},{1... | collective-permute-start | bytes 1572872 | tf_op jit(solution)/shard_map/ppermute | solution.py:236
  106.0 9.3 %collective-permute-start.20 = (f32[128,1024]{1,0:T(8,128)S(1)}, f32[128,1024]{1,0:T(8,128)S(1)}, u32[]{:S(2)}, u32[]{:S(2)}) collective-permute-start(f32[128,1024]{1,0:T(8,128)S(1)} %pad_maximum_fusion.2.refs_0_), channel_id=1, source_target_pairs={{0,32},{16,112},{32,0},{48,80},{64,96},{80,48},{96,64},{112,16},{1... | collective-permute-start | bytes 1572872 | tf_op jit(solution)/shard_map/ppermute | solution.py:236
  107.3 8.1 %collective-permute-start.21 = (f32[128,1024]{1,0:T(8,128)S(1)}, f32[128,1024]{1,0:T(8,128)S(1)}, u32[]{:S(2)}, u32[]{:S(2)}) collective-permute-start(f32[128,1024]{1,0:T(8,128)S(1)} %pad_maximum_fusion.2.refs_0_), channel_id=1, source_target_pairs={{0,16},{16,0},{32,48},{48,32},{64,80},{80,64},{96,112},{112,96},{1... | collective-permute-start | bytes 1572872 | tf_op jit(solution)/shard_map/ppermute | solution.py:236
  115.3 1.9 %collective-permute-start.22 = (f32[128,1024]{1,0:T(8,128)S(1)}, f32[128,1024]{1,0:T(8,128)S(1)}, u32[]{:S(2)}, u32[]{:S(2)}) collective-permute-start(f32[128,1024]{1,0:T(8,128)S(1)} %collective-permute-done.20.refs_1_), channel_id=1, source_target_pairs={{0,16},{16,0},{32,48},{48,32},{64,80},{80,64},{96,112},{112,96},{1... | collective-permute-start | bytes 1572872 | tf_op jit(solution)/shard_map/ppermute | solution.py:236
where the time goes:
time: 125 us
  Pallas kernels  47.3 us (38%)
  starting transfers between devices  44.3 us (35%)
  waiting for transfers between devices  30.8 us (25%)
    ppermute x15, starting transfers between devices, swap(): return lax.ppermute(a, 'row', pairs)  29.6 us
    ppermute x15, waiting for transfers between devices, swap(): return lax.ppermute(a, 'row', pairs)  18.5 us
    pallas_call x4, Pallas kernels, factor_rows(): pl.pallas_call(functools.partial(factor_kernel, k, nb), out_shape=jax.Sha...  16 us
    pallas_call x2, Pallas kernels, finish(): pl.pallas_call(functools.partial(finish_kernel, first), out_shape=(jax.Sh...  15 us
    ppermute x8, starting transfers between devices, gather_panel(): lax.ppermute(h, ('row', 'col'), gather_pairs(q, step))  14.7 us
    ppermute x8, waiting for transfers between devices, gather_panel(): lax.ppermute(h, ('row', 'col'), gather_pairs(q, step))  12.3 us
    pallas_call x2, Pallas kernels, share(): pl.pallas_call(functools.partial(share_kernel, first), out_shape=(half, h...  9.04 us
    pallas_call x1, Pallas kernels, gram_share(): pl.pallas_call(gram_kernel, out_shape=(half, half), in_specs=whole(), out...  3.1 us
  transfers between devices with their start and end apart: 23, of which 15 were waited for; matrix products, arithmetic and copies ran while one was open for 0% of the time, Pallas kernels for 28%

commit v1 on v0

--- a/solution.py
+++ b/solution.py
@@ -282,26 +282,6 @@
     )(hi, lo, trailing)
 
 
-def fold_kernel(k0, k1, g0, g1, keep_ref, give_ref):
-    n = k0.shape[1]
-    for cols, k, g in ((slice(0, n), k0, g0), (slice(n, 2 * n), k1, g1)):
-        give_ref[:, cols] = k[128:, :] + g[128:, :]
-        keep_ref[:, cols] = k[:128, :] + g[:128, :]
-
-
-def fold(keeps, gots):
-    out = jax.ShapeDtypeStruct((128, 2 * keeps[0].shape[1]), F32)
-    return pl.pallas_call(
-        fold_kernel,
-        out_shape=(out, out),
-        in_specs=whole(4),
-        out_specs=whole(2),
-        compiler_params=params(28),
-        cost_estimate=cheap(),
-        name="fold",
-    )(*keeps, *gots)
-
-
 def prepare_kernel(w0, w1, w2, w3, p_ref, r_ref, ihi_ref, ilo_ref, bhi_ref, blo_ref, inv):
     ri = lax.broadcasted_iota(jnp.int32, (128, 128), 0)
     ci = lax.broadcasted_iota(jnp.int32, (128, 128), 1)
@@ -419,27 +399,34 @@
     second = share(after(hi, gram, first[0]), lo, trailing, width, width)
     gram = gram + came
     second, gram = lax.optimization_barrier((second, gram))
-    keep, give = fold((first[0], second[0]), [swap(g, CORE) for g in (first[1], second[1])])
-
-    x_came = swap(give, ROW[0])
+
+    keeps, gives = [], []
+    for keep, give in (first, second):
+        got = swap(give, CORE)
+        gives.append(keep[128:] + got[128:])
+        keeps.append(keep[:128] + got[:128])
+    came = [swap(g, ROW[0]) for g in gives]
     packed = (gram, swap(gram, CORE))
-    factors = [factor_rows(0, 4, [], packed)]
-    factors.append(factor_rows(1, 4, factors, packed))
-    keep, came, factors = lax.optimization_barrier((keep, x_came, factors))
-    give, keep = keep[64:] + came[64:], keep[:64] + came[:64]
-    came = swap(give, ROW[1])
-    factors.append(factor_rows(2, 4, factors, packed))
-    factors.append(factor_rows(3, 4, factors, packed))
-    own, factors = lax.optimization_barrier((keep + came, factors))
-    came = swap(own, ROW[1])
-    r_factor, ihi, ilo, bhi, blo = prepare(factors, rows)
-    own, came, ihi = lax.optimization_barrier((own, came, ihi))
-    done = ()
-    own = [jnp.concatenate([own[:, at:at + width], came[:, at:at + width]], axis=0) for at in (0, width)]
+    factors = []
+    for c in (0, 1):
+        factors.append(factor_rows(c, 4, factors, packed))
+        came[c], keeps[c], factors[-1] = lax.optimization_barrier((came[c], keeps[c], factors[-1]))
+        give, keeps[c] = keeps[c][64:] + came[c][64:], keeps[c][:64] + came[c][:64]
+        came[c] = swap(give, ROW[1])
+    own = []
+    for c in (0, 1):
+        factors.append(factor_rows(2 + c, 4, factors, packed))
+        came[c], keeps[c], factors[-1] = lax.optimization_barrier((came[c], keeps[c], factors[-1]))
+        own.append(keeps[c] + came[c])
+        came[c] = swap(own[c], ROW[1])
+    r_factor, ihi, ilo, bhi, blo = prepare(factors, after(rows, own[1]))
+    own[0], came[0], ihi = lax.optimization_barrier((own[0], came[0], ihi))
+    own = [jnp.concatenate(p, axis=0) for p in zip(own, came)]
     came = [swap(own[0], ROW[0])]
     own[1] = after(own[1], came[0])
     came.append(swap(own[1], ROW[0]))
     own_across = [swap(p, CORE) for p in own]
+    done = ()
     for c in (0, 1):
         pieces = [own[c], came[c], own_across[c], swap(came[c], CORE)]
         done = finish(pieces, ihi, ilo, bhi, blo, trailing, c * width, done)

time: 125 us -> 120 us (0.960)
  waiting for transfers between devices: 30.8 us -> 27.2 us
  starting transfers between devices: 44.3 us -> 42.6 us
    ppermute x15 -> x18, waiting for transfers between devices: 18.5 us -> 14.9 us  [swap(): return lax.ppermute(a, 'row', pairs)]
    ppermute x15 -> x18, starting transfers between devices: 29.6 us -> 27.9 us  [swap(): return lax.ppermute(a, 'row', pairs)]
  transfers between devices with their start and end apart: 23 -> 26, of which waited for: 15 -> 13; matrix products, arithmetic and copies ran while one was open for 0% -> 1% of each run, Pallas kernels for 28% -> 30%
where the time goes in v1:
time: 120 us
  Pallas kernels  47.1 us (39%)
  starting transfers between devices  42.6 us (36%)
  waiting for transfers between devices  27.2 us (23%)
    ppermute x18, starting transfers between devices, swap(): return lax.ppermute(a, 'row', pairs)  27.9 us
    pallas_call x4, Pallas kernels, factor_rows(): pl.pallas_call(functools.partial(factor_kernel, k, nb), out_shape=jax.Sha...  16 us
    pallas_call x2, Pallas kernels, finish(): pl.pallas_call(functools.partial(finish_kernel, first), out_shape=(jax.Sh...  15 us
    ppermute x18, waiting for transfers between devices, swap(): return lax.ppermute(a, 'row', pairs)  14.9 us
    ppermute x8, starting transfers between devices, gather_panel(): lax.ppermute(h, ('row', 'col'), gather_pairs(q, step))  14.7 us
    ppermute x8, waiting for transfers between devices, gather_panel(): lax.ppermute(h, ('row', 'col'), gather_pairs(q, step))  12.3 us
    pallas_call x2, Pallas kernels, share(): pl.pallas_call(functools.partial(share_kernel, first), out_shape=(half, h...  9.04 us
    pallas_call x1, Pallas kernels, gram_share(): pl.pallas_call(gram_kernel, out_shape=(half, half), in_specs=whole(), out...  3.1 us
  transfers between devices with their start and end apart: 26, of which 13 were waited for; matrix products, arithmetic and copies ran while one was open for 1% of the time, Pallas kernels for 30%

profile of v1, /device:TPU:1, one launch (start us, length us, event | category | flops | bytes accessed | tf_op | source)
XLA Modules:
  0.0 119.7 jit_solution(2323455102098528919)
XLA Ops:
  0.6 0.9 fusion
  1.5 2.2 %collective-permute-start = (f32[64,256]{1,0:T(8,128)S(1)}, f32[64,256]{1,0:T(8,128)S(1)}, u32[]{:S(2)}, u32[]{:S(2)}) collective-permute-start(f32[64,256]{1,0:T(8,128)S(1)} %get-tuple-element.100), channel_id=1, source_target_pairs={{0,1},{1,0},{2,3},{3,2},{4,5},{5,4},{6,7},{7,6},{8,9},{9,8},{10,11... | collective-permute-start | bytes 196616 | tf_op jit(solution)/shard_map/ppermute | solution.py:179
  3.7 1.9 %collective-permute-start.4 = (f32[64,256]{1,0:T(8,128)S(1)}, f32[64,256]{1,0:T(8,128)S(1)}, u32[]{:S(2)}, u32[]{:S(2)}) collective-permute-start(f32[64,256]{1,0:T(8,128)S(1)} %get-tuple-element.99), channel_id=1, source_target_pairs={{0,3},{1,2},{2,1},{3,0},{4,7},{5,6},{6,5},{7,4},{8,11},{9,10},{10,... | collective-permute-start | bytes 196616 | tf_op jit(solution)/shard_map/ppermute | solution.py:179
  5.6 2.7 %collective-permute-start.1 = (f32[128,256]{1,0:T(8,128)S(1)}, f32[128,256]{1,0:T(8,128)S(1)}, u32[]{:S(2)}, u32[]{:S(2)}) collective-permute-start(f32[128,256]{1,0:T(8,128)S(1)} %pad_maximum_fusion.5), channel_id=1, source_target_pairs={{0,3},{1,2},{2,1},{3,0},{4,7},{5,6},{6,5},{7,4},{8,11},{9,10},{10,... | collective-permute-start | bytes 393224 | tf_op jit(solution)/shard_map/ppermute | solution.py:179
  8.4 0.1 collective-permute-start.5
  8.5 2.3 %collective-permute-done.1 = f32[128,256]{1,0:T(8,128)S(1)} collective-permute-done((f32[128,256]{1,0:T(8,128)S(1)}, f32[128,256]{1,0:T(8,128)S(1)}, u32[]{:S(2)}, u32[]{:S(2)}) %collective-permute-start.1) | collective-permute-done | bytes 131104 | tf_op jit(solution)/shard_map/ppermute | solution.py:179
  10.8 1.7 %collective-permute-start.2 = (f32[256,256]{1,0:T(8,128)S(1)}, f32[256,256]{1,0:T(8,128)S(1)}, u32[]{:S(2)}, u32[]{:S(2)}) collective-permute-start(f32[256,256]{1,0:T(8,128)S(1)} %pad_maximum_fusion.3), channel_id=1, source_target_pairs={{0,4},{1,5},{2,6},{3,7},{4,0},{5,1},{6,2},{7,3},{8,12},{9,13},{10,... | collective-permute-start | bytes 786440 | tf_op jit(solution)/shard_map/ppermute | solution.py:179
  12.5 3.9 %collective-permute-start.6 = (f32[256,256]{1,0:T(8,128)S(1)}, f32[256,256]{1,0:T(8,128)S(1)}, u32[]{:S(2)}, u32[]{:S(2)}) collective-permute-start(f32[256,256]{1,0:T(8,128)S(1)} %pad_maximum_fusion.4), channel_id=1, source_target_pairs={{0,12},{1,13},{2,14},{3,15},{4,8},{5,9},{6,10},{7,11},{8,4},{9,5},... | collective-permute-start | bytes 786440 | tf_op jit(solution)/shard_map/ppermute | solution.py:179
  16.4 1.5 %collective-permute-done.2 = f32[256,256]{1,0:T(8,128)S(1)} collective-permute-done((f32[256,256]{1,0:T(8,128)S(1)}, f32[256,256]{1,0:T(8,128)S(1)}, u32[]{:S(2)}, u32[]{:S(2)}) %collective-permute-start.2) | collective-permute-done | bytes 262176 | tf_op jit(solution)/shard_map/ppermute | solution.py:179
  18.0 2.0 %collective-permute-start.3 = (f32[512,256]{1,0:T(8,128)S(1)}, f32[512,256]{1,0:T(8,128)S(1)}, u32[]{:S(2)}, u32[]{:S(2)}) collective-permute-start(f32[512,256]{1,0:T(8,128)S(1)} %pad_maximum_fusion.refs_0_), channel_id=1, source_target_pairs={{0,12},{1,13},{2,14},{3,15},{4,8},{5,9},{6,10},{7,11},{8,4},{9,5},... | collective-permute-start | bytes 1572872 | tf_op jit(solution)/shard_map/ppermute | solution.py:179
  20.0 0.2 collective-permute-done.6
  20.2 0.1 collective-permute-start.7
  20.3 7.3 %collective-permute-done.3.refs_1_ = f32[512,256]{1,0:T(8,128)S(1)} collective-permute-done((f32[512,256]{1,0:T(8,128)S(1)}, f32[512,256]{1,0:T(8,128)S(1)}, u32[]{:S(2)}, u32[]{:S(2)}) %collective-permute-start.3) | collective-permute-done | bytes 524320 | tf_op jit(solution)/shard_map/ppermute | solution.py:179
  27.6 1.0 collective-permute-done.7.refs_3_
  28.6 0.9 turn.1
  29.6 3.1 %gram.1 = (f32[640,128]{1,0:T(8,128)S(1)}, f32[640,128]{1,0:T(8,128)S(1)}) custom-call(f32[1024,512]{1,0:T(8,128)S(1)} %get-tuple-element.72.p_ref), custom_call_target="tpu_custom_call" | custom-call | flops 3000000000 | bytes 10000000 | tf_op jit(solution)/shard_map/gram/pallas_call | solution.py:223
  32.7 6.4 %collective-permute-start.8 = (f32[640,128]{1,0:T(8,128)S(1)}, f32[640,128]{1,0:T(8,128)S(1)}, u32[]{:S(2)}, u32[]{:S(2)}) collective-permute-start(f32[640,128]{1,0:T(8,128)S(1)} %get-tuple-element.50), channel_id=1, source_target_pairs={{0,16},{16,0},{32,48},{48,32},{64,80},{80,64},{96,112},{112,96},{1... | collective-permute-start | bytes 983048 | tf_op jit(solution)/shard_map/ppermute | solution.py:236
  39.1 1.3 %collective-permute-done.8 = f32[640,128]{1,0:T(8,128)S(1)} collective-permute-done((f32[640,128]{1,0:T(8,128)S(1)}, f32[640,128]{1,0:T(8,128)S(1)}, u32[]{:S(2)}, u32[]{:S(2)}) %collective-permute-start.8) | collective-permute-done | bytes 327712 | tf_op jit(solution)/shard_map/ppermute | solution.py:236
  40.4 2.6 %collective-permute-start.11 = (f32[640,128]{1,0:T(8,128)S(1)}, f32[640,128]{1,0:T(8,128)S(1)}, u32[]{:S(2)}, u32[]{:S(2)}) collective-permute-start(f32[640,128]{1,0:T(8,128)S(1)} %add.39), channel_id=1, source_target_pairs={{0,32},{16,112},{32,0},{48,80},{64,96},{80,48},{96,64},{112,16},{1... | collective-permute-start | bytes 983048 | tf_op jit(solution)/shard_map/ppermute | solution.py:236
  42.9 4.5 %share.2 = (f32[256,1024]{1,0:T(8,128)S(1)}, f32[256,1024]{1,0:T(8,128)S(1)}) custom-call(bf16[512,1024]{1,0:T(8,128)(2,1)S(1)} %get-tuple-element.56.hi_ref, bf16[512,1024]{1,0:T(8,128)(2,1)S(1)} %get-tuple-element.52.lo_ref, f32[1024,2048]{1,0:T(8,128)S(1)} %bitcast.1), custom_call_target="tpu_custom_call" | custom-call | flops 3000000000 | bytes 10000000 | tf_op jit(solution)/shard_map/share/pallas_call | solution.py:269
  47.5 0.1 collective-permute-done.11
  47.6 0.4 collective-permute-start.12
  48.0 2.8 %collective-permute-start.9 = (f32[256,1024]{1,0:T(8,128)S(1)}, f32[256,1024]{1,0:T(8,128)S(1)}, u32[]{:S(2)}, u32[]{:S(2)}) collective-permute-start(f32[256,1024]{1,0:T(8,128)S(1)} %get-tuple-element.54), channel_id=1, source_target_pairs={{0,16},{16,0},{32,48},{48,32},{64,80},{80,64},{96,112},{112,96},{1... | collective-permute-start | bytes 3145736 | tf_op jit(solution)/shard_map/ppermute | solution.py:236
  50.8 4.5 %share.3 = (f32[256,1024]{1,0:T(8,128)S(1)}, f32[256,1024]{1,0:T(8,128)S(1)}) custom-call(bf16[512,1024]{1,0:T(8,128)(2,1)S(1)} %get-tuple-element.56.hi_ref, bf16[512,1024]{1,0:T(8,128)(2,1)S(1)} %get-tuple-element.52.lo_ref, f32[1024,2048]{1,0:T(8,128)S(1)} %bitcast.1), custom_call_target="tpu_custom_call" | custom-call | flops 3000000000 | bytes 10000000 | tf_op jit(solution)/shard_map/share/pallas_call | solution.py:269
  55.3 1.1 collective-permute-start.14
  56.4 0.2 slice_add_fusion.2
  56.6 2.6 %collective-permute-start.10 = (f32[128,1024]{1,0:T(8,128)S(1)}, f32[128,1024]{1,0:T(8,128)S(1)}, u32[]{:S(2)}, u32[]{:S(2)}) collective-permute-start(f32[128,1024]{1,0:T(8,128)S(1)} %get-tuple-element.94), channel_id=1, source_target_pairs={{0,32},{16,112},{32,0},{48,80},{64,96},{80,48},{96,64},{112,16},{1... | collective-permute-start | bytes 1572872 | tf_op jit(solution)/shard_map/ppermute | solution.py:236
  59.2 0.2 slice_add_fusion
  59.3 2.3 %collective-permute-start.15 = (f32[128,1024]{1,0:T(8,128)S(1)}, f32[128,1024]{1,0:T(8,128)S(1)}, u32[]{:S(2)}, u32[]{:S(2)}) collective-permute-start(f32[128,1024]{1,0:T(8,128)S(1)} %get-tuple-element.92), channel_id=1, source_target_pairs={{0,32},{16,112},{32,0},{48,80},{64,96},{80,48},{96,64},{112,16},{1... | collective-permute-start | bytes 1572872 | tf_op jit(solution)/shard_map/ppermute | solution.py:236
  61.6 3.6 %factor.4.refs_0_.w0 = f32[128,640]{1,0:T(8,128)S(1)} custom-call(f32[640,128]{1,0:T(8,128)S(1)} %add.43.refs_0_.refs_1_.refs_2_.refs_3_, f32[640,128]{1,0:T(8,128)S(1)} %collective-permute-done.13.refs_1_.refs_2_.refs_3_.refs_4_), custom_call_target="tpu_custom_call" | custom-call | flops 300000000 | bytes 1000000 | tf_op jit(solution)/shard_map/factor/pallas_call | solution.py:150
  65.3 0.7 collective-permute-done.10
  66.1 4.0 %factor.5.refs_1_.w1 = f32[128,640]{1,0:T(8,128)S(1)} custom-call(f32[128,640]{1,0:T(8,128)S(1)} %factor.4.refs_0_.w0, f32[640,128]{1,0:T(8,128)S(1)} %add.43.refs_0_.refs_1_.refs_2_.refs_3_, f32[640,128]{1,0:T(8,128)S(1)} %collective-permute-done.13.refs_1_.refs_2_.refs_3_.refs_4_), custom_call_target="tpu_custom_call" | custom-call | flops 300000000 | bytes 1000000 | tf_op jit(solution)/shard_map/factor/pallas_call | solution.py:150
  70.1 3.1 %collective-permute-done.15 = f32[128,1024]{1,0:T(8,128)S(1)} collective-permute-done((f32[128,1024]{1,0:T(8,128)S(1)}, f32[128,1024]{1,0:T(8,128)S(1)}, u32[]{:S(2)}, u32[]{:S(2)}) %collective-permute-start.15) | collective-permute-done | bytes 524320 | tf_op jit(solution)/shard_map/ppermute | solution.py:236
  73.3 4.1 %factor.6.refs_2_.w2 = f32[128,640]{1,0:T(8,128)S(1)} custom-call(f32[128,640]{1,0:T(8,128)S(1)} %factor.4.refs_0_.w0, f32[128,640]{1,0:T(8,128)S(1)} %factor.5.refs_1_.w1, f32[640,128]{1,0:T(8,128)S(1)} %add.43.refs_0_.refs_1_.refs_2_.refs_3_, f32[640,128]{1,0:T(8,128)S(1)} %collective-permute-done.13.refs_1_.refs_2_.refs_3_.refs_4_), custom_call_target="tpu_custom_call" | custom-call | flops 300000000 | bytes 1000000 | tf_op jit(solution)/shard_map/factor/pallas_call | solution.py:150
  77.5 1.7 %collective-permute-start.19 = (f32[64,1024]{1,0:T(8,128)S(1)}, f32[64,1024]{1,0:T(8,128)S(1)}, u32[]{:S(2)}, u32[]{:S(2)}) collective-permute-start(f32[64,1024]{1,0:T(8,128)S(1)} %add.51), channel_id=1, source_target_pairs={{0,96},{16,48},{32,64},{48,16},{64,32},{80,112},{96,0},{112,80},{1... | collective-permute-start | bytes 786440 | tf_op jit(solution)/shard_map/ppermute | solution.py:236
  79.3 4.2 %factor.7.w3 = f32[128,640]{1,0:T(8,128)S(1)} custom-call(f32[128,640]{1,0:T(8,128)S(1)} %factor.4.refs_0_.w0, f32[128,640]{1,0:T(8,128)S(1)} %factor.5.refs_1_.w1, f32[128,640]{1,0:T(8,128)S(1)} %factor.6.refs_2_.w2, f32[640,128]{1,0:T(8,128)S(1)} %add.43.refs_0_.refs_1_.refs_2_.refs_3_, f32[640,128]{1,0:T(8,128)S(1)} %collective-permute-done.13.refs_1_.refs_2_.refs_3_.refs_4_), custom_call_target="tpu_custom_call" | custom-call | flops 300000000 | bytes 1000000 | tf_op jit(solution)/shard_map/factor/pallas_call | solution.py:150
  83.5 3.0 %prepare.1 = (f32[512,512]{1,0:T(8,128)}, bf16[512,512]{1,0:T(8,128)(2,1)S(1)}, bf16[512,512]{1,0:T(8,128)(2,1)S(1)}, bf16[1024,512]{1,0:T(8,128)(2,1)S(1)}, bf16[1024,512]{1,0:T(8,128)(2,1)S(1)}) custom-call(f32[128,640]{1,0:T(8,128)S(1)} %factor.4.refs_0_.w0, f32[128,640]{1,0:T(8,128)S(1)} %factor.5.refs_1_.w1, f32[128,640]{1,0:T(8,128)S(1)} %factor.6.refs_2_.w2, ...), custom_call_target="tpu_custom_call" | custom-call | flops 300000000 | bytes 1000000 | tf_op jit(solution)/shard_map/prepare/pallas_call | solution.py:309
  86.6 2.6 %collective-permute-start.20 = (f32[128,1024]{1,0:T(8,128)S(1)}, f32[128,1024]{1,0:T(8,128)S(1)}, u32[]{:S(2)}, u32[]{:S(2)}) collective-permute-start(f32[128,1024]{1,0:T(8,128)S(1)} %constant_dynamic-update-slice_fusion.refs_0_), channel_id=1, source_target_pairs={{0,32},{16,112},{32,0},{48,80},{64,96},{80,48},{96,64},{112,16},{1... | collective-permute-start | bytes 1572872 | tf_op jit(solution)/shard_map/ppermute | solution.py:236
  89.2 2.7 %collective-permute-start.21 = (f32[128,1024]{1,0:T(8,128)S(1)}, f32[128,1024]{1,0:T(8,128)S(1)}, u32[]{:S(2)}, u32[]{:S(2)}) collective-permute-start(f32[128,1024]{1,0:T(8,128)S(1)} %constant_dynamic-update-slice_fusion.refs_0_), channel_id=1, source_target_pairs={{0,16},{16,0},{32,48},{48,32},{64,80},{80,64},{96,112},{112,96},{1... | collective-permute-start | bytes 1572872 | tf_op jit(solution)/shard_map/ppermute | solution.py:236
  91.9 7.0 %collective-permute-done.20.refs_1_ = f32[128,1024]{1,0:T(8,128)S(1)} collective-permute-done((f32[128,1024]{1,0:T(8,128)S(1)}, f32[128,1024]{1,0:T(8,128)S(1)}, u32[]{:S(2)}, u32[]{:S(2)}) %collective-permute-start.20) | collective-permute-done | bytes 524320 | tf_op jit(solution)/shard_map/ppermute | solution.py:236
  98.9 1.8 %collective-permute-start.22 = (f32[128,1024]{1,0:T(8,128)S(1)}, f32[128,1024]{1,0:T(8,128)S(1)}, u32[]{:S(2)}, u32[]{:S(2)}) collective-permute-start(f32[128,1024]{1,0:T(8,128)S(1)} %collective-permute-done.20.refs_1_), channel_id=1, source_target_pairs={{0,16},{16,0},{32,48},{48,32},{64,80},{80,64},{96,112},{112,96},{1... | collective-permute-start | bytes 1572872 | tf_op jit(solution)/shard_map/ppermute | solution.py:236
  100.8 0.8 collective-permute-start.23
  101.5 0.7 collective-permute-done.22.refs_3_
  102.2 7.5 %finish.2 = (f32[512,2048]{1,0:T(8,128)}, f32[1024,2048]{1,0:T(8,128)}) custom-call(f32[128,1024]{1,0:T(8,128)S(1)} %constant_dynamic-update-slice_fusion.refs_0_, f32[128,1024]{1,0:T(8,128)S(1)} %collective-permute-done.20.refs_1_, f32[128,1024]{1,0:T(8,128)S(1)} %collective-permute-done.21.refs_2_, f32[128,1024]{1,0:T(8,128)S(1)} %collective-permute-done.22.refs_3_, ...), custom_call_target="tpu_custom_call" | custom-call | flops 300000000 | bytes 1000000 | tf_op jit(solution)/shard_map/finish/pallas_call | solution.py:365
  109.8 0.3 collective-permute-done.23.refs_1_
  110.1 0.1 collective-permute-start.25
  110.2 1.8 %collective-permute-done.25.refs_3_ = f32[128,1024]{1,0:T(8,128)S(1)} collective-permute-done((f32[128,1024]{1,0:T(8,128)S(1)}, f32[128,1024]{1,0:T(8,128)S(1)}, u32[]{:S(2)}, u32[]{:S(2)}) %collective-permute-start.25) | collective-permute-done | bytes 524320 | tf_op jit(solution)/shard_map/ppermute | solution.py:236
  112.0 7.5 %finish.3 = (f32[512,2048]{1,0:T(8,128)}, f32[1024,2048]{1,0:T(8,128)}) custom-call(f32[128,1024]{1,0:T(8,128)S(1)} %pad_maximum_fusion.2.refs_0_, f32[128,1024]{1,0:T(8,128)S(1)} %collective-permute-done.23.refs_1_, f32[128,1024]{1,0:T(8,128)S(1)} %collective-permute-done.24.refs_2_, ...), custom_call_target="tpu_custom_call", output_to_operand_aliasing={{0}: (9, {}), {1}: (10, {})} | custom-call | flops 300000000 | bytes 1000000 | tf_op jit(solution)/shard_map/finish/pallas_call | solution.py:365
  (39 shorter events, 0.7 us)
Async XLA Ops:
  1.5 4.1 %collective-permute-start = (f32[64,256]{1,0:T(8,128)S(1)}, f32[64,256]{1,0:T(8,128)S(1)}, u32[]{:S(2)}, u32[]{:S(2)}) collective-permute-start(f32[64,256]{1,0:T(8,128)S(1)} %get-tuple-element.100), channel_id=1, source_target_pairs={{0,1},{1,0},{2,3},{3,2},{4,5},{5,4},{6,7},{7,6},{8,9},{9,8},{10,11... | collective-permute-start | bytes 196616 | tf_op jit(solution)/shard_map/ppermute | solution.py:179
  3.7 4.7 %collective-permute-start.4 = (f32[64,256]{1,0:T(8,128)S(1)}, f32[64,256]{1,0:T(8,128)S(1)}, u32[]{:S(2)}, u32[]{:S(2)}) collective-permute-start(f32[64,256]{1,0:T(8,128)S(1)} %get-tuple-element.99), channel_id=1, source_target_pairs={{0,3},{1,2},{2,1},{3,0},{4,7},{5,6},{6,5},{7,4},{8,11},{9,10},{10,... | collective-permute-start | bytes 196616 | tf_op jit(solution)/shard_map/ppermute | solution.py:179
  5.6 5.1 %collective-permute-start.1 = (f32[128,256]{1,0:T(8,128)S(1)}, f32[128,256]{1,0:T(8,128)S(1)}, u32[]{:S(2)}, u32[]{:S(2)}) collective-permute-start(f32[128,256]{1,0:T(8,128)S(1)} %pad_maximum_fusion.5), channel_id=1, source_target_pairs={{0,3},{1,2},{2,1},{3,0},{4,7},{5,6},{6,5},{7,4},{8,11},{9,10},{10,... | collective-permute-start | bytes 393224 | tf_op jit(solution)/shard_map/ppermute | solution.py:179
  8.4 4.1 %collective-permute-start.5 = (f32[128,256]{1,0:T(8,128)S(1)}, f32[128,256]{1,0:T(8,128)S(1)}, u32[]{:S(2)}, u32[]{:S(2)}) collective-permute-start(f32[128,256]{1,0:T(8,128)S(1)} %pad_maximum_fusion.6), channel_id=1, source_target_pairs={{0,1},{1,0},{2,3},{3,2},{4,5},{5,4},{6,7},{7,6},{8,9},{9,8},{10,11... | collective-permute-start | bytes 393224 | tf_op jit(solution)/shard_map/ppermute | solution.py:179
  10.8 7.2 %collective-permute-start.2 = (f32[256,256]{1,0:T(8,128)S(1)}, f32[256,256]{1,0:T(8,128)S(1)}, u32[]{:S(2)}, u32[]{:S(2)}) collective-permute-start(f32[256,256]{1,0:T(8,128)S(1)} %pad_maximum_fusion.3), channel_id=1, source_target_pairs={{0,4},{1,5},{2,6},{3,7},{4,0},{5,1},{6,2},{7,3},{8,12},{9,13},{10,... | collective-permute-start | bytes 786440 | tf_op jit(solution)/shard_map/ppermute | solution.py:179
  12.5 7.7 %collective-permute-start.6 = (f32[256,256]{1,0:T(8,128)S(1)}, f32[256,256]{1,0:T(8,128)S(1)}, u32[]{:S(2)}, u32[]{:S(2)}) collective-permute-start(f32[256,256]{1,0:T(8,128)S(1)} %pad_maximum_fusion.4), channel_id=1, source_target_pairs={{0,12},{1,13},{2,14},{3,15},{4,8},{5,9},{6,10},{7,11},{8,4},{9,5},... | collective-permute-start | bytes 786440 | tf_op jit(solution)/shard_map/ppermute | solution.py:179
  18.0 9.6 %collective-permute-start.3 = (f32[512,256]{1,0:T(8,128)S(1)}, f32[512,256]{1,0:T(8,128)S(1)}, u32[]{:S(2)}, u32[]{:S(2)}) collective-permute-start(f32[512,256]{1,0:T(8,128)S(1)} %pad_maximum_fusion.refs_0_), channel_id=1, source_target_pairs={{0,12},{1,13},{2,14},{3,15},{4,8},{5,9},{6,10},{7,11},{8,4},{9,5},... | collective-permute-start | bytes 1572872 | tf_op jit(solution)/shard_map/ppermute | solution.py:179
  20.2 8.4 %collective-permute-start.7 = (f32[512,256]{1,0:T(8,128)S(1)}, f32[512,256]{1,0:T(8,128)S(1)}, u32[]{:S(2)}, u32[]{:S(2)}) collective-permute-start(f32[512,256]{1,0:T(8,128)S(1)} %pad_maximum_fusion.1.refs_2_), channel_id=1, source_target_pairs={{0,4},{1,5},{2,6},{3,7},{4,0},{5,1},{6,2},{7,3},{8,12},{9,13},{10,... | collective-permute-start | bytes 1572872 | tf_op jit(solution)/shard_map/ppermute | solution.py:179
  28.6 14.3 %slice-start = ((s8[8388608]{0:T(1024)(128)(4,1)}), s8[4194304]{0:T(1024)(128)(4,1)S(1)}, s32[]{:S(2)}) async-start(s8[8388608]{0:T(1024)(128)(4,1)} %bitcast), calls=%async_computation | async-start | bytes 8388608
  29.6 13.4 %slice-start.1 = ((s8[8388608]{0:T(1024)(128)(4,1)}), s8[4194304]{0:T(1024)(128)(4,1)S(1)}, s32[]{:S(2)}) async-start(s8[8388608]{0:T(1024)(128)(4,1)} %bitcast), calls=%async_computation.1 | async-start | bytes 8388608
  32.7 7.6 %collective-permute-start.8 = (f32[640,128]{1,0:T(8,128)S(1)}, f32[640,128]{1,0:T(8,128)S(1)}, u32[]{:S(2)}, u32[]{:S(2)}) collective-permute-start(f32[640,128]{1,0:T(8,128)S(1)} %get-tuple-element.50), channel_id=1, source_target_pairs={{0,16},{16,0},{32,48},{48,32},{64,80},{80,64},{96,112},{112,96},{1... | collective-permute-start | bytes 983048 | tf_op jit(solution)/shard_map/ppermute | solution.py:236
  40.4 7.2 %collective-permute-start.11 = (f32[640,128]{1,0:T(8,128)S(1)}, f32[640,128]{1,0:T(8,128)S(1)}, u32[]{:S(2)}, u32[]{:S(2)}) collective-permute-start(f32[640,128]{1,0:T(8,128)S(1)} %add.39), channel_id=1, source_target_pairs={{0,32},{16,112},{32,0},{48,80},{64,96},{80,48},{96,64},{112,16},{1... | collective-permute-start | bytes 983048 | tf_op jit(solution)/shard_map/ppermute | solution.py:236
  47.6 7.7 %collective-permute-start.12 = (f32[640,128]{1,0:T(8,128)S(1)}, f32[640,128]{1,0:T(8,128)S(1)}, u32[]{:S(2)}, u32[]{:S(2)}) collective-permute-start(f32[640,128]{1,0:T(8,128)S(1)} %add.42), channel_id=1, source_target_pairs={{0,96},{16,48},{32,64},{48,16},{64,32},{80,112},{96,0},{112,80},{1... | collective-permute-start | bytes 983048 | tf_op jit(solution)/shard_map/ppermute | solution.py:236
  48.0 8.4 %collective-permute-start.9 = (f32[256,1024]{1,0:T(8,128)S(1)}, f32[256,1024]{1,0:T(8,128)S(1)}, u32[]{:S(2)}, u32[]{:S(2)}) collective-permute-start(f32[256,1024]{1,0:T(8,128)S(1)} %get-tuple-element.54), channel_id=1, source_target_pairs={{0,16},{16,0},{32,48},{48,32},{64,80},{80,64},{96,112},{112,96},{1... | collective-permute-start | bytes 3145736 | tf_op jit(solution)/shard_map/ppermute | solution.py:236
  55.3 3.8 %collective-permute-start.14 = (f32[256,1024]{1,0:T(8,128)S(1)}, f32[256,1024]{1,0:T(8,128)S(1)}, u32[]{:S(2)}, u32[]{:S(2)}) collective-permute-start(f32[256,1024]{1,0:T(8,128)S(1)} %get-tuple-element.62), channel_id=1, source_target_pairs={{0,16},{16,0},{32,48},{48,32},{64,80},{80,64},{96,112},{112,96},{1... | collective-permute-start | bytes 3145736 | tf_op jit(solution)/shard_map/ppermute | solution.py:236
  56.6 9.3 %collective-permute-start.10 = (f32[128,1024]{1,0:T(8,128)S(1)}, f32[128,1024]{1,0:T(8,128)S(1)}, u32[]{:S(2)}, u32[]{:S(2)}) collective-permute-start(f32[128,1024]{1,0:T(8,128)S(1)} %get-tuple-element.94), channel_id=1, source_target_pairs={{0,32},{16,112},{32,0},{48,80},{64,96},{80,48},{96,64},{112,16},{1... | collective-permute-start | bytes 1572872 | tf_op jit(solution)/shard_map/ppermute | solution.py:236
  59.2 2.5 %collective-permute-start.13 = (f32[640,128]{1,0:T(8,128)S(1)}, f32[640,128]{1,0:T(8,128)S(1)}, u32[]{:S(2)}, u32[]{:S(2)}) collective-permute-start(f32[640,128]{1,0:T(8,128)S(1)} %add.43.refs_0_.refs_1_.refs_2_.refs_3_), channel_id=1, source_target_pairs={{0,16},{16,0},{32,48},{48,32},{64,80},{80,64},{96,112},{112,96},{1... | collective-permute-start | bytes 983048 | tf_op jit(solution)/shard_map/ppermute | solution.py:236
  59.3 13.8 %collective-permute-start.15 = (f32[128,1024]{1,0:T(8,128)S(1)}, f32[128,1024]{1,0:T(8,128)S(1)}, u32[]{:S(2)}, u32[]{:S(2)}) collective-permute-start(f32[128,1024]{1,0:T(8,128)S(1)} %get-tuple-element.92), channel_id=1, source_target_pairs={{0,32},{16,112},{32,0},{48,80},{64,96},{80,48},{96,64},{112,16},{1... | collective-permute-start | bytes 1572872 | tf_op jit(solution)/shard_map/ppermute | solution.py:236
  66.0 11.5 %collective-permute-start.16 = (f32[64,1024]{1,0:T(8,128)S(1)}, f32[64,1024]{1,0:T(8,128)S(1)}, u32[]{:S(2)}, u32[]{:S(2)}) collective-permute-start(f32[64,1024]{1,0:T(8,128)S(1)} %get-tuple-element.98), channel_id=1, source_target_pairs={{0,96},{16,48},{32,64},{48,16},{64,32},{80,112},{96,0},{112,80},{1... | collective-permute-start | bytes 786440 | tf_op jit(solution)/shard_map/ppermute | solution.py:236
  73.3 10.2 %collective-permute-start.17 = (f32[64,1024]{1,0:T(8,128)S(1)}, f32[64,1024]{1,0:T(8,128)S(1)}, u32[]{:S(2)}, u32[]{:S(2)}) collective-permute-start(f32[64,1024]{1,0:T(8,128)S(1)} %get-tuple-element.96), channel_id=1, source_target_pairs={{0,96},{16,48},{32,64},{48,16},{64,32},{80,112},{96,0},{112,80},{1... | collective-permute-start | bytes 786440 | tf_op jit(solution)/shard_map/ppermute | solution.py:236
  77.5 9.0 %collective-permute-start.19 = (f32[64,1024]{1,0:T(8,128)S(1)}, f32[64,1024]{1,0:T(8,128)S(1)}, u32[]{:S(2)}, u32[]{:S(2)}) collective-permute-start(f32[64,1024]{1,0:T(8,128)S(1)} %add.51), channel_id=1, source_target_pairs={{0,96},{16,48},{32,64},{48,16},{64,32},{80,112},{96,0},{112,80},{1... | collective-permute-start | bytes 786440 | tf_op jit(solution)/shard_map/ppermute | solution.py:236
  86.6 12.3 %collective-permute-start.20 = (f32[128,1024]{1,0:T(8,128)S(1)}, f32[128,1024]{1,0:T(8,128)S(1)}, u32[]{:S(2)}, u32[]{:S(2)}) collective-permute-start(f32[128,1024]{1,0:T(8,128)S(1)} %constant_dynamic-update-slice_fusion.refs_0_), channel_id=1, source_target_pairs={{0,32},{16,112},{32,0},{48,80},{64,96},{80,48},{96,64},{112,16},{1... | collective-permute-start | bytes 1572872 | tf_op jit(solution)/shard_map/ppermute | solution.py:236
  89.2 11.5 %collective-permute-start.18 = (f32[64,1024]{1,0:T(8,128)S(1)}, f32[64,1024]{1,0:T(8,128)S(1)}, u32[]{:S(2)}, u32[]{:S(2)}) collective-permute-start(f32[64,1024]{1,0:T(8,128)S(1)} %add.50), channel_id=1, source_target_pairs={{0,96},{16,48},{32,64},{48,16},{64,32},{80,112},{96,0},{112,80},{1... | collective-permute-start | bytes 786440 | tf_op jit(solution)/shard_map/ppermute | solution.py:236
  89.2 12.3 %collective-permute-start.21 = (f32[128,1024]{1,0:T(8,128)S(1)}, f32[128,1024]{1,0:T(8,128)S(1)}, u32[]{:S(2)}, u32[]{:S(2)}) collective-permute-start(f32[128,1024]{1,0:T(8,128)S(1)} %constant_dynamic-update-slice_fusion.refs_0_), channel_id=1, source_target_pairs={{0,16},{16,0},{32,48},{48,32},{64,80},{80,64},{96,112},{112,96},{1... | collective-permute-start | bytes 1572872 | tf_op jit(solution)/shard_map/ppermute | solution.py:236
  98.9 3.4 %collective-permute-start.22 = (f32[128,1024]{1,0:T(8,128)S(1)}, f32[128,1024]{1,0:T(8,128)S(1)}, u32[]{:S(2)}, u32[]{:S(2)}) collective-permute-start(f32[128,1024]{1,0:T(8,128)S(1)} %collective-permute-done.20.refs_1_), channel_id=1, source_target_pairs={{0,16},{16,0},{32,48},{48,32},{64,80},{80,64},{96,112},{112,96},{1... | collective-permute-start | bytes 1572872 | tf_op jit(solution)/shard_map/ppermute | solution.py:236
  100.8 9.3 %collective-permute-start.23 = (f32[128,1024]{1,0:T(8,128)S(1)}, f32[128,1024]{1,0:T(8,128)S(1)}, u32[]{:S(2)}, u32[]{:S(2)}) collective-permute-start(f32[128,1024]{1,0:T(8,128)S(1)} %pad_maximum_fusion.2.refs_0_), channel_id=1, source_target_pairs={{0,32},{16,112},{32,0},{48,80},{64,96},{80,48},{96,64},{112,16},{1... | collective-permute-start | bytes 1572872 | tf_op jit(solution)/shard_map/ppermute | solution.py:236
  101.5 8.7 %collective-permute-start.24 = (f32[128,1024]{1,0:T(8,128)S(1)}, f32[128,1024]{1,0:T(8,128)S(1)}, u32[]{:S(2)}, u32[]{:S(2)}) collective-permute-start(f32[128,1024]{1,0:T(8,128)S(1)} %pad_maximum_fusion.2.refs_0_), channel_id=1, source_target_pairs={{0,16},{16,0},{32,48},{48,32},{64,80},{80,64},{96,112},{112,96},{1... | collective-permute-start | bytes 1572872 | tf_op jit(solution)/shard_map/ppermute | solution.py:236
  110.1 1.9 %collective-permute-start.25 = (f32[128,1024]{1,0:T(8,128)S(1)}, f32[128,1024]{1,0:T(8,128)S(1)}, u32[]{:S(2)}, u32[]{:S(2)}) collective-permute-start(f32[128,1024]{1,0:T(8,128)S(1)} %collective-permute-done.23.refs_1_), channel_id=1, source_target_pairs={{0,16},{16,0},{32,48},{48,32},{64,80},{80,64},{96,112},{112,96},{1... | collective-permute-start | bytes 1572872 | tf_op jit(solution)/shard_map/ppermute | solution.py:236

commit v2 on v1

--- a/solution.py
+++ b/solution.py
@@ -420,7 +420,7 @@
         own.append(keeps[c] + came[c])
         came[c] = swap(own[c], ROW[1])
     r_factor, ihi, ilo, bhi, blo = prepare(factors, after(rows, own[1]))
-    own[0], came[0], ihi = lax.optimization_barrier((own[0], came[0], ihi))
+    own, came, ihi = lax.optimization_barrier((own, came, ihi))
     own = [jnp.concatenate(p, axis=0) for p in zip(own, came)]
     came = [swap(own[0], ROW[0])]
     own[1] = after(own[1], came[0])

time: 120 us -> 123 us (1.025)
  starting transfers between devices: 42.6 us -> 47.4 us
  waiting for transfers between devices: 27.2 us -> 25.6 us
    ppermute x18, starting transfers between devices: 27.9 us -> 32.7 us  [swap(): return lax.ppermute(a, 'row', pairs)]
    ppermute x18, waiting for transfers between devices: 14.9 us -> 13.4 us  [swap(): return lax.ppermute(a, 'row', pairs)]
  transfers between devices with their start and end apart: 26 -> 26, of which waited for: 13 -> 12; matrix products, arithmetic and copies ran while one was open for 1% -> 1% of each run, Pallas kernels for 30% -> 29%
where the time goes in v2:
time: 123 us
  starting transfers between devices  47.4 us (39%)
  Pallas kernels  47.1 us (38%)
  waiting for transfers between devices  25.6 us (21%)
    ppermute x18, starting transfers between devices, swap(): return lax.ppermute(a, 'row', pairs)  32.7 us
    pallas_call x4, Pallas kernels, factor_rows(): pl.pallas_call(functools.partial(factor_kernel, k, nb), out_shape=jax.Sha...  16 us
    pallas_call x2, Pallas kernels, finish(): pl.pallas_call(functools.partial(finish_kernel, first), out_shape=(jax.Sh...  15.1 us
    ppermute x8, starting transfers between devices, gather_panel(): lax.ppermute(h, ('row', 'col'), gather_pairs(q, step))  14.7 us
    ppermute x18, waiting for transfers between devices, swap(): return lax.ppermute(a, 'row', pairs)  13.4 us
    ppermute x8, waiting for transfers between devices, gather_panel(): lax.ppermute(h, ('row', 'col'), gather_pairs(q, step))  12.3 us
    pallas_call x2, Pallas kernels, share(): pl.pallas_call(functools.partial(share_kernel, first), out_shape=(half, h...  9.04 us
    pallas_call x1, Pallas kernels, gram_share(): pl.pallas_call(gram_kernel, out_shape=(half, half), in_specs=whole(), out...  3.1 us
  transfers between devices with their start and end apart: 26, of which 12 were waited for; matrix products, arithmetic and copies ran while one was open for 1% of the time, Pallas kernels for 29%

profile of v2, /device:TPU:1, one launch (start us, length us, event | category | flops | bytes accessed | tf_op | source)
XLA Modules:
  0.0 123.0 jit_solution(207523668583069857)
XLA Ops:
  0.6 0.9 fusion
  1.5 2.2 %collective-permute-start = (f32[64,256]{1,0:T(8,128)S(1)}, f32[64,256]{1,0:T(8,128)S(1)}, u32[]{:S(2)}, u32[]{:S(2)}) collective-permute-start(f32[64,256]{1,0:T(8,128)S(1)} %get-tuple-element.104), channel_id=1, source_target_pairs={{0,1},{1,0},{2,3},{3,2},{4,5},{5,4},{6,7},{7,6},{8,9},{9,8},{10,11... | collective-permute-start | bytes 196616 | tf_op jit(solution)/shard_map/ppermute | solution.py:179
  3.7 1.9 %collective-permute-start.4 = (f32[64,256]{1,0:T(8,128)S(1)}, f32[64,256]{1,0:T(8,128)S(1)}, u32[]{:S(2)}, u32[]{:S(2)}) collective-permute-start(f32[64,256]{1,0:T(8,128)S(1)} %get-tuple-element.103), channel_id=1, source_target_pairs={{0,3},{1,2},{2,1},{3,0},{4,7},{5,6},{6,5},{7,4},{8,11},{9,10},{10,... | collective-permute-start | bytes 196616 | tf_op jit(solution)/shard_map/ppermute | solution.py:179
  5.6 2.7 %collective-permute-start.1 = (f32[128,256]{1,0:T(8,128)S(1)}, f32[128,256]{1,0:T(8,128)S(1)}, u32[]{:S(2)}, u32[]{:S(2)}) collective-permute-start(f32[128,256]{1,0:T(8,128)S(1)} %pad_maximum_fusion.5), channel_id=1, source_target_pairs={{0,3},{1,2},{2,1},{3,0},{4,7},{5,6},{6,5},{7,4},{8,11},{9,10},{10,... | collective-permute-start | bytes 393224 | tf_op jit(solution)/shard_map/ppermute | solution.py:179
  8.4 0.1 collective-permute-start.5
  8.5 2.3 %collective-permute-done.1 = f32[128,256]{1,0:T(8,128)S(1)} collective-permute-done((f32[128,256]{1,0:T(8,128)S(1)}, f32[128,256]{1,0:T(8,128)S(1)}, u32[]{:S(2)}, u32[]{:S(2)}) %collective-permute-start.1) | collective-permute-done | bytes 131104 | tf_op jit(solution)/shard_map/ppermute | solution.py:179
  10.8 1.7 %collective-permute-start.2 = (f32[256,256]{1,0:T(8,128)S(1)}, f32[256,256]{1,0:T(8,128)S(1)}, u32[]{:S(2)}, u32[]{:S(2)}) collective-permute-start(f32[256,256]{1,0:T(8,128)S(1)} %pad_maximum_fusion.3), channel_id=1, source_target_pairs={{0,4},{1,5},{2,6},{3,7},{4,0},{5,1},{6,2},{7,3},{8,12},{9,13},{10,... | collective-permute-start | bytes 786440 | tf_op jit(solution)/shard_map/ppermute | solution.py:179
  12.5 3.9 %collective-permute-start.6 = (f32[256,256]{1,0:T(8,128)S(1)}, f32[256,256]{1,0:T(8,128)S(1)}, u32[]{:S(2)}, u32[]{:S(2)}) collective-permute-start(f32[256,256]{1,0:T(8,128)S(1)} %pad_maximum_fusion.4), channel_id=1, source_target_pairs={{0,12},{1,13},{2,14},{3,15},{4,8},{5,9},{6,10},{7,11},{8,4},{9,5},... | collective-permute-start | bytes 786440 | tf_op jit(solution)/shard_map/ppermute | solution.py:179
  16.4 1.5 %collective-permute-done.2 = f32[256,256]{1,0:T(8,128)S(1)} collective-permute-done((f32[256,256]{1,0:T(8,128)S(1)}, f32[256,256]{1,0:T(8,128)S(1)}, u32[]{:S(2)}, u32[]{:S(2)}) %collective-permute-start.2) | collective-permute-done | bytes 262176 | tf_op jit(solution)/shard_map/ppermute | solution.py:179
  18.0 2.0 %collective-permute-start.3 = (f32[512,256]{1,0:T(8,128)S(1)}, f32[512,256]{1,0:T(8,128)S(1)}, u32[]{:S(2)}, u32[]{:S(2)}) collective-permute-start(f32[512,256]{1,0:T(8,128)S(1)} %pad_maximum_fusion.refs_0_), channel_id=1, source_target_pairs={{0,12},{1,13},{2,14},{3,15},{4,8},{5,9},{6,10},{7,11},{8,4},{9,5},... | collective-permute-start | bytes 1572872 | tf_op jit(solution)/shard_map/ppermute | solution.py:179
  20.0 0.2 collective-permute-done.6
  20.2 0.1 collective-permute-start.7
  20.3 7.3 %collective-permute-done.3.refs_1_ = f32[512,256]{1,0:T(8,128)S(1)} collective-permute-done((f32[512,256]{1,0:T(8,128)S(1)}, f32[512,256]{1,0:T(8,128)S(1)}, u32[]{:S(2)}, u32[]{:S(2)}) %collective-permute-start.3) | collective-permute-done | bytes 524320 | tf_op jit(solution)/shard_map/ppermute | solution.py:179
  27.6 1.0 collective-permute-done.7.refs_3_
  28.6 0.9 turn.1
  29.6 3.1 %gram.1 = (f32[640,128]{1,0:T(8,128)S(1)}, f32[640,128]{1,0:T(8,128)S(1)}) custom-call(f32[1024,512]{1,0:T(8,128)S(1)} %get-tuple-element.74.p_ref), custom_call_target="tpu_custom_call" | custom-call | flops 3000000000 | bytes 10000000 | tf_op jit(solution)/shard_map/gram/pallas_call | solution.py:223
  32.7 6.4 %collective-permute-start.8 = (f32[640,128]{1,0:T(8,128)S(1)}, f32[640,128]{1,0:T(8,128)S(1)}, u32[]{:S(2)}, u32[]{:S(2)}) collective-permute-start(f32[640,128]{1,0:T(8,128)S(1)} %get-tuple-element.52), channel_id=1, source_target_pairs={{0,16},{16,0},{32,48},{48,32},{64,80},{80,64},{96,112},{112,96},{1... | collective-permute-start | bytes 983048 | tf_op jit(solution)/shard_map/ppermute | solution.py:236
  39.1 1.3 %collective-permute-done.8 = f32[640,128]{1,0:T(8,128)S(1)} collective-permute-done((f32[640,128]{1,0:T(8,128)S(1)}, f32[640,128]{1,0:T(8,128)S(1)}, u32[]{:S(2)}, u32[]{:S(2)}) %collective-permute-start.8) | collective-permute-done | bytes 327712 | tf_op jit(solution)/shard_map/ppermute | solution.py:236
  40.4 2.6 %collective-permute-start.11 = (f32[640,128]{1,0:T(8,128)S(1)}, f32[640,128]{1,0:T(8,128)S(1)}, u32[]{:S(2)}, u32[]{:S(2)}) collective-permute-start(f32[640,128]{1,0:T(8,128)S(1)} %add.39), channel_id=1, source_target_pairs={{0,32},{16,112},{32,0},{48,80},{64,96},{80,48},{96,64},{112,16},{1... | collective-permute-start | bytes 983048 | tf_op jit(solution)/shard_map/ppermute | solution.py:236
  42.9 4.5 %share.2 = (f32[256,1024]{1,0:T(8,128)S(1)}, f32[256,1024]{1,0:T(8,128)S(1)}) custom-call(bf16[512,1024]{1,0:T(8,128)(2,1)S(1)} %get-tuple-element.58.hi_ref, bf16[512,1024]{1,0:T(8,128)(2,1)S(1)} %get-tuple-element.54.lo_ref, f32[1024,2048]{1,0:T(8,128)S(1)} %bitcast.1), custom_call_target="tpu_custom_call" | custom-call | flops 3000000000 | bytes 10000000 | tf_op jit(solution)/shard_map/share/pallas_call | solution.py:269
  47.5 0.1 collective-permute-done.11
  47.6 0.4 collective-permute-start.12
  48.0 2.8 %collective-permute-start.9 = (f32[256,1024]{1,0:T(8,128)S(1)}, f32[256,1024]{1,0:T(8,128)S(1)}, u32[]{:S(2)}, u32[]{:S(2)}) collective-permute-start(f32[256,1024]{1,0:T(8,128)S(1)} %get-tuple-element.56), channel_id=1, source_target_pairs={{0,16},{16,0},{32,48},{48,32},{64,80},{80,64},{96,112},{112,96},{1... | collective-permute-start | bytes 3145736 | tf_op jit(solution)/shard_map/ppermute | solution.py:236
  50.8 4.5 %share.3 = (f32[256,1024]{1,0:T(8,128)S(1)}, f32[256,1024]{1,0:T(8,128)S(1)}) custom-call(bf16[512,1024]{1,0:T(8,128)(2,1)S(1)} %get-tuple-element.58.hi_ref, bf16[512,1024]{1,0:T(8,128)(2,1)S(1)} %get-tuple-element.54.lo_ref, f32[1024,2048]{1,0:T(8,128)S(1)} %bitcast.1), custom_call_target="tpu_custom_call" | custom-call | flops 3000000000 | bytes 10000000 | tf_op jit(solution)/shard_map/share/pallas_call | solution.py:269
  55.3 1.1 collective-permute-start.14
  56.4 0.2 slice_add_fusion.2
  56.6 2.6 %collective-permute-start.10 = (f32[128,1024]{1,0:T(8,128)S(1)}, f32[128,1024]{1,0:T(8,128)S(1)}, u32[]{:S(2)}, u32[]{:S(2)}) collective-permute-start(f32[128,1024]{1,0:T(8,128)S(1)} %get-tuple-element.98), channel_id=1, source_target_pairs={{0,32},{16,112},{32,0},{48,80},{64,96},{80,48},{96,64},{112,16},{1... | collective-permute-start | bytes 1572872 | tf_op jit(solution)/shard_map/ppermute | solution.py:236
  59.2 0.2 slice_add_fusion
  59.3 2.3 %collective-permute-start.15 = (f32[128,1024]{1,0:T(8,128)S(1)}, f32[128,1024]{1,0:T(8,128)S(1)}, u32[]{:S(2)}, u32[]{:S(2)}) collective-permute-start(f32[128,1024]{1,0:T(8,128)S(1)} %get-tuple-element.96), channel_id=1, source_target_pairs={{0,32},{16,112},{32,0},{48,80},{64,96},{80,48},{96,64},{112,16},{1... | collective-permute-start | bytes 1572872 | tf_op jit(solution)/shard_map/ppermute | solution.py:236
  61.6 3.6 %factor.4.refs_0_.w0 = f32[128,640]{1,0:T(8,128)S(1)} custom-call(f32[640,128]{1,0:T(8,128)S(1)} %add.43.refs_0_.refs_1_.refs_2_.refs_3_, f32[640,128]{1,0:T(8,128)S(1)} %collective-permute-done.13.refs_1_.refs_2_.refs_3_.refs_4_), custom_call_target="tpu_custom_call" | custom-call | flops 300000000 | bytes 1000000 | tf_op jit(solution)/shard_map/factor/pallas_call | solution.py:150
  65.3 0.7 collective-permute-done.10
  66.1 4.0 %factor.5.refs_1_.w1 = f32[128,640]{1,0:T(8,128)S(1)} custom-call(f32[128,640]{1,0:T(8,128)S(1)} %factor.4.refs_0_.w0, f32[640,128]{1,0:T(8,128)S(1)} %add.43.refs_0_.refs_1_.refs_2_.refs_3_, f32[640,128]{1,0:T(8,128)S(1)} %collective-permute-done.13.refs_1_.refs_2_.refs_3_.refs_4_), custom_call_target="tpu_custom_call" | custom-call | flops 300000000 | bytes 1000000 | tf_op jit(solution)/shard_map/factor/pallas_call | solution.py:150
  70.1 3.1 %collective-permute-done.15 = f32[128,1024]{1,0:T(8,128)S(1)} collective-permute-done((f32[128,1024]{1,0:T(8,128)S(1)}, f32[128,1024]{1,0:T(8,128)S(1)}, u32[]{:S(2)}, u32[]{:S(2)}) %collective-permute-start.15) | collective-permute-done | bytes 524320 | tf_op jit(solution)/shard_map/ppermute | solution.py:236
  73.3 4.1 %factor.6.refs_2_.w2 = f32[128,640]{1,0:T(8,128)S(1)} custom-call(f32[128,640]{1,0:T(8,128)S(1)} %factor.4.refs_0_.w0, f32[128,640]{1,0:T(8,128)S(1)} %factor.5.refs_1_.w1, f32[640,128]{1,0:T(8,128)S(1)} %add.43.refs_0_.refs_1_.refs_2_.refs_3_, f32[640,128]{1,0:T(8,128)S(1)} %collective-permute-done.13.refs_1_.refs_2_.refs_3_.refs_4_), custom_call_target="tpu_custom_call" | custom-call | flops 300000000 | bytes 1000000 | tf_op jit(solution)/shard_map/factor/pallas_call | solution.py:150
  77.5 1.7 %collective-permute-start.18 = (f32[64,1024]{1,0:T(8,128)S(1)}, f32[64,1024]{1,0:T(8,128)S(1)}, u32[]{:S(2)}, u32[]{:S(2)}) collective-permute-start(f32[64,1024]{1,0:T(8,128)S(1)} %add.51), channel_id=1, source_target_pairs={{0,96},{16,48},{32,64},{48,16},{64,32},{80,112},{96,0},{112,80},{1... | collective-permute-start | bytes 786440 | tf_op jit(solution)/shard_map/ppermute | solution.py:236
  79.3 4.2 %factor.7.w3 = f32[128,640]{1,0:T(8,128)S(1)} custom-call(f32[128,640]{1,0:T(8,128)S(1)} %factor.4.refs_0_.w0, f32[128,640]{1,0:T(8,128)S(1)} %factor.5.refs_1_.w1, f32[128,640]{1,0:T(8,128)S(1)} %factor.6.refs_2_.w2, f32[640,128]{1,0:T(8,128)S(1)} %add.43.refs_0_.refs_1_.refs_2_.refs_3_, f32[640,128]{1,0:T(8,128)S(1)} %collective-permute-done.13.refs_1_.refs_2_.refs_3_.refs_4_), custom_call_target="tpu_custom_call" | custom-call | flops 300000000 | bytes 1000000 | tf_op jit(solution)/shard_map/factor/pallas_call | solution.py:150
  83.5 0.1 collective-permute-start.19
  83.6 3.0 %prepare.1 = (f32[512,512]{1,0:T(8,128)}, bf16[512,512]{1,0:T(8,128)(2,1)S(1)}, bf16[512,512]{1,0:T(8,128)(2,1)S(1)}, bf16[1024,512]{1,0:T(8,128)(2,1)S(1)}, bf16[1024,512]{1,0:T(8,128)(2,1)S(1)}) custom-call(f32[128,640]{1,0:T(8,128)S(1)} %factor.4.refs_0_.w0, f32[128,640]{1,0:T(8,128)S(1)} %factor.5.refs_1_.w1, f32[128,640]{1,0:T(8,128)S(1)} %factor.6.refs_2_.w2, ...), custom_call_target="tpu_custom_call" | custom-call | flops 300000000 | bytes 1000000 | tf_op jit(solution)/shard_map/prepare/pallas_call | solution.py:309
  86.7 2.2 %collective-permute-done.19 = f32[64,1024]{1,0:T(8,128)S(1)} collective-permute-done((f32[64,1024]{1,0:T(8,128)S(1)}, f32[64,1024]{1,0:T(8,128)S(1)}, u32[]{:S(2)}, u32[]{:S(2)}) %collective-permute-start.19) | collective-permute-done | bytes 262176 | tf_op jit(solution)/shard_map/ppermute | solution.py:236
  88.9 2.6 %collective-permute-start.20 = (f32[128,1024]{1,0:T(8,128)S(1)}, f32[128,1024]{1,0:T(8,128)S(1)}, u32[]{:S(2)}, u32[]{:S(2)}) collective-permute-start(f32[128,1024]{1,0:T(8,128)S(1)} %constant_dynamic-update-slice_fusion.refs_0_), channel_id=1, source_target_pairs={{0,32},{16,112},{32,0},{48,80},{64,96},{80,48},{96,64},{112,16},{1... | collective-permute-start | bytes 1572872 | tf_op jit(solution)/shard_map/ppermute | solution.py:236
  91.5 2.5 %collective-permute-start.21 = (f32[128,1024]{1,0:T(8,128)S(1)}, f32[128,1024]{1,0:T(8,128)S(1)}, u32[]{:S(2)}, u32[]{:S(2)}) collective-permute-start(f32[128,1024]{1,0:T(8,128)S(1)} %constant_dynamic-update-slice_fusion.refs_0_), channel_id=1, source_target_pairs={{0,16},{16,0},{32,48},{48,32},{64,80},{80,64},{96,112},{112,96},{1... | collective-permute-start | bytes 1572872 | tf_op jit(solution)/shard_map/ppermute | solution.py:236
  93.9 4.5 %collective-permute-done.20.refs_1_ = f32[128,1024]{1,0:T(8,128)S(1)} collective-permute-done((f32[128,1024]{1,0:T(8,128)S(1)}, f32[128,1024]{1,0:T(8,128)S(1)}, u32[]{:S(2)}, u32[]{:S(2)}) %collective-permute-start.20) | collective-permute-done | bytes 524320 | tf_op jit(solution)/shard_map/ppermute | solution.py:236
  98.5 4.6 %collective-permute-start.22 = (f32[128,1024]{1,0:T(8,128)S(1)}, f32[128,1024]{1,0:T(8,128)S(1)}, u32[]{:S(2)}, u32[]{:S(2)}) collective-permute-start(f32[128,1024]{1,0:T(8,128)S(1)} %collective-permute-done.20.refs_1_), channel_id=1, source_target_pairs={{0,16},{16,0},{32,48},{48,32},{64,80},{80,64},{96,112},{112,96},{1... | collective-permute-start | bytes 1572872 | tf_op jit(solution)/shard_map/ppermute | solution.py:236
  103.1 2.6 %collective-permute-start.23 = (f32[128,1024]{1,0:T(8,128)S(1)}, f32[128,1024]{1,0:T(8,128)S(1)}, u32[]{:S(2)}, u32[]{:S(2)}) collective-permute-start(f32[128,1024]{1,0:T(8,128)S(1)} %pad_maximum_fusion.2.refs_0_), channel_id=1, source_target_pairs={{0,32},{16,112},{32,0},{48,80},{64,96},{80,48},{96,64},{112,16},{1... | collective-permute-start | bytes 1572872 | tf_op jit(solution)/shard_map/ppermute | solution.py:236
  105.7 7.5 %finish.2 = (f32[512,2048]{1,0:T(8,128)}, f32[1024,2048]{1,0:T(8,128)}) custom-call(f32[128,1024]{1,0:T(8,128)S(1)} %constant_dynamic-update-slice_fusion.refs_0_, f32[128,1024]{1,0:T(8,128)S(1)} %collective-permute-done.20.refs_1_, f32[128,1024]{1,0:T(8,128)S(1)} %collective-permute-done.21.refs_2_, f32[128,1024]{1,0:T(8,128)S(1)} %collective-permute-done.22.refs_3_, ...), custom_call_target="tpu_custom_call" | custom-call | flops 300000000 | bytes 1000000 | tf_op jit(solution)/shard_map/finish/pallas_call | solution.py:365
  113.2 0.6 collective-permute-start.25
  113.8 1.5 %collective-permute-done.25.refs_3_ = f32[128,1024]{1,0:T(8,128)S(1)} collective-permute-done((f32[128,1024]{1,0:T(8,128)S(1)}, f32[128,1024]{1,0:T(8,128)S(1)}, u32[]{:S(2)}, u32[]{:S(2)}) %collective-permute-start.25) | collective-permute-done | bytes 524320 | tf_op jit(solution)/shard_map/ppermute | solution.py:236
  115.3 7.5 %finish.3 = (f32[512,2048]{1,0:T(8,128)}, f32[1024,2048]{1,0:T(8,128)}) custom-call(f32[128,1024]{1,0:T(8,128)S(1)} %pad_maximum_fusion.2.refs_0_, f32[128,1024]{1,0:T(8,128)S(1)} %collective-permute-done.23.refs_1_, f32[128,1024]{1,0:T(8,128)S(1)} %collective-permute-done.24.refs_2_, ...), custom_call_target="tpu_custom_call", output_to_operand_aliasing={{0}: (9, {}), {1}: (10, {})} | custom-call | flops 300000000 | bytes 1000000 | tf_op jit(solution)/shard_map/finish/pallas_call | solution.py:365
  (39 shorter events, 0.7 us)
Async XLA Ops:
  1.5 4.1 %collective-permute-start = (f32[64,256]{1,0:T(8,128)S(1)}, f32[64,256]{1,0:T(8,128)S(1)}, u32[]{:S(2)}, u32[]{:S(2)}) collective-permute-start(f32[64,256]{1,0:T(8,128)S(1)} %get-tuple-element.104), channel_id=1, source_target_pairs={{0,1},{1,0},{2,3},{3,2},{4,5},{5,4},{6,7},{7,6},{8,9},{9,8},{10,11... | collective-permute-start | bytes 196616 | tf_op jit(solution)/shard_map/ppermute | solution.py:179
  3.7 4.7 %collective-permute-start.4 = (f32[64,256]{1,0:T(8,128)S(1)}, f32[64,256]{1,0:T(8,128)S(1)}, u32[]{:S(2)}, u32[]{:S(2)}) collective-permute-start(f32[64,256]{1,0:T(8,128)S(1)} %get-tuple-element.103), channel_id=1, source_target_pairs={{0,3},{1,2},{2,1},{3,0},{4,7},{5,6},{6,5},{7,4},{8,11},{9,10},{10,... | collective-permute-start | bytes 196616 | tf_op jit(solution)/shard_map/ppermute | solution.py:179
  5.6 5.1 %collective-permute-start.1 = (f32[128,256]{1,0:T(8,128)S(1)}, f32[128,256]{1,0:T(8,128)S(1)}, u32[]{:S(2)}, u32[]{:S(2)}) collective-permute-start(f32[128,256]{1,0:T(8,128)S(1)} %pad_maximum_fusion.5), channel_id=1, source_target_pairs={{0,3},{1,2},{2,1},{3,0},{4,7},{5,6},{6,5},{7,4},{8,11},{9,10},{10,... | collective-permute-start | bytes 393224 | tf_op jit(solution)/shard_map/ppermute | solution.py:179
  8.4 4.1 %collective-permute-start.5 = (f32[128,256]{1,0:T(8,128)S(1)}, f32[128,256]{1,0:T(8,128)S(1)}, u32[]{:S(2)}, u32[]{:S(2)}) collective-permute-start(f32[128,256]{1,0:T(8,128)S(1)} %pad_maximum_fusion.6), channel_id=1, source_target_pairs={{0,1},{1,0},{2,3},{3,2},{4,5},{5,4},{6,7},{7,6},{8,9},{9,8},{10,11... | collective-permute-start | bytes 393224 | tf_op jit(solution)/shard_map/ppermute | solution.py:179
  10.8 7.2 %collective-permute-start.2 = (f32[256,256]{1,0:T(8,128)S(1)}, f32[256,256]{1,0:T(8,128)S(1)}, u32[]{:S(2)}, u32[]{:S(2)}) collective-permute-start(f32[256,256]{1,0:T(8,128)S(1)} %pad_maximum_fusion.3), channel_id=1, source_target_pairs={{0,4},{1,5},{2,6},{3,7},{4,0},{5,1},{6,2},{7,3},{8,12},{9,13},{10,... | collective-permute-start | bytes 786440 | tf_op jit(solution)/shard_map/ppermute | solution.py:179
  12.5 7.7 %collective-permute-start.6 = (f32[256,256]{1,0:T(8,128)S(1)}, f32[256,256]{1,0:T(8,128)S(1)}, u32[]{:S(2)}, u32[]{:S(2)}) collective-permute-start(f32[256,256]{1,0:T(8,128)S(1)} %pad_maximum_fusion.4), channel_id=1, source_target_pairs={{0,12},{1,13},{2,14},{3,15},{4,8},{5,9},{6,10},{7,11},{8,4},{9,5},... | collective-permute-start | bytes 786440 | tf_op jit(solution)/shard_map/ppermute | solution.py:179
  18.0 9.6 %collective-permute-start.3 = (f32[512,256]{1,0:T(8,128)S(1)}, f32[512,256]{1,0:T(8,128)S(1)}, u32[]{:S(2)}, u32[]{:S(2)}) collective-permute-start(f32[512,256]{1,0:T(8,128)S(1)} %pad_maximum_fusion.refs_0_), channel_id=1, source_target_pairs={{0,12},{1,13},{2,14},{3,15},{4,8},{5,9},{6,10},{7,11},{8,4},{9,5},... | collective-permute-start | bytes 1572872 | tf_op jit(solution)/shard_map/ppermute | solution.py:179
  20.2 8.4 %collective-permute-start.7 = (f32[512,256]{1,0:T(8,128)S(1)}, f32[512,256]{1,0:T(8,128)S(1)}, u32[]{:S(2)}, u32[]{:S(2)}) collective-permute-start(f32[512,256]{1,0:T(8,128)S(1)} %pad_maximum_fusion.1.refs_2_), channel_id=1, source_target_pairs={{0,4},{1,5},{2,6},{3,7},{4,0},{5,1},{6,2},{7,3},{8,12},{9,13},{10,... | collective-permute-start | bytes 1572872 | tf_op jit(solution)/shard_map/ppermute | solution.py:179
  28.6 14.3 %slice-start = ((s8[8388608]{0:T(1024)(128)(4,1)}), s8[4194304]{0:T(1024)(128)(4,1)S(1)}, s32[]{:S(2)}) async-start(s8[8388608]{0:T(1024)(128)(4,1)} %bitcast), calls=%async_computation | async-start | bytes 8388608
  29.6 13.4 %slice-start.1 = ((s8[8388608]{0:T(1024)(128)(4,1)}), s8[4194304]{0:T(1024)(128)(4,1)S(1)}, s32[]{:S(2)}) async-start(s8[8388608]{0:T(1024)(128)(4,1)} %bitcast), calls=%async_computation.1 | async-start | bytes 8388608
  32.7 7.6 %collective-permute-start.8 = (f32[640,128]{1,0:T(8,128)S(1)}, f32[640,128]{1,0:T(8,128)S(1)}, u32[]{:S(2)}, u32[]{:S(2)}) collective-permute-start(f32[640,128]{1,0:T(8,128)S(1)} %get-tuple-element.52), channel_id=1, source_target_pairs={{0,16},{16,0},{32,48},{48,32},{64,80},{80,64},{96,112},{112,96},{1... | collective-permute-start | bytes 983048 | tf_op jit(solution)/shard_map/ppermute | solution.py:236
  40.4 7.2 %collective-permute-start.11 = (f32[640,128]{1,0:T(8,128)S(1)}, f32[640,128]{1,0:T(8,128)S(1)}, u32[]{:S(2)}, u32[]{:S(2)}) collective-permute-start(f32[640,128]{1,0:T(8,128)S(1)} %add.39), channel_id=1, source_target_pairs={{0,32},{16,112},{32,0},{48,80},{64,96},{80,48},{96,64},{112,16},{1... | collective-permute-start | bytes 983048 | tf_op jit(solution)/shard_map/ppermute | solution.py:236
  47.6 7.7 %collective-permute-start.12 = (f32[640,128]{1,0:T(8,128)S(1)}, f32[640,128]{1,0:T(8,128)S(1)}, u32[]{:S(2)}, u32[]{:S(2)}) collective-permute-start(f32[640,128]{1,0:T(8,128)S(1)} %add.42), channel_id=1, source_target_pairs={{0,96},{16,48},{32,64},{48,16},{64,32},{80,112},{96,0},{112,80},{1... | collective-permute-start | bytes 983048 | tf_op jit(solution)/shard_map/ppermute | solution.py:236
  48.0 8.4 %collective-permute-start.9 = (f32[256,1024]{1,0:T(8,128)S(1)}, f32[256,1024]{1,0:T(8,128)S(1)}, u32[]{:S(2)}, u32[]{:S(2)}) collective-permute-start(f32[256,1024]{1,0:T(8,128)S(1)} %get-tuple-element.56), channel_id=1, source_target_pairs={{0,16},{16,0},{32,48},{48,32},{64,80},{80,64},{96,112},{112,96},{1... | collective-permute-start | bytes 3145736 | tf_op jit(solution)/shard_map/ppermute | solution.py:236
  55.3 3.8 %collective-permute-start.14 = (f32[256,1024]{1,0:T(8,128)S(1)}, f32[256,1024]{1,0:T(8,128)S(1)}, u32[]{:S(2)}, u32[]{:S(2)}) collective-permute-start(f32[256,1024]{1,0:T(8,128)S(1)} %get-tuple-element.64), channel_id=1, source_target_pairs={{0,16},{16,0},{32,48},{48,32},{64,80},{80,64},{96,112},{112,96},{1... | collective-permute-start | bytes 3145736 | tf_op jit(solution)/shard_map/ppermute | solution.py:236
  56.6 9.3 %collective-permute-start.10 = (f32[128,1024]{1,0:T(8,128)S(1)}, f32[128,1024]{1,0:T(8,128)S(1)}, u32[]{:S(2)}, u32[]{:S(2)}) collective-permute-start(f32[128,1024]{1,0:T(8,128)S(1)} %get-tuple-element.98), channel_id=1, source_target_pairs={{0,32},{16,112},{32,0},{48,80},{64,96},{80,48},{96,64},{112,16},{1... | collective-permute-start | bytes 1572872 | tf_op jit(solution)/shard_map/ppermute | solution.py:236
  59.2 2.5 %collective-permute-start.13 = (f32[640,128]{1,0:T(8,128)S(1)}, f32[640,128]{1,0:T(8,128)S(1)}, u32[]{:S(2)}, u32[]{:S(2)}) collective-permute-start(f32[640,128]{1,0:T(8,128)S(1)} %add.43.refs_0_.refs_1_.refs_2_.refs_3_), channel_id=1, source_target_pairs={{0,16},{16,0},{32,48},{48,32},{64,80},{80,64},{96,112},{112,96},{1... | collective-permute-start | bytes 983048 | tf_op jit(solution)/shard_map/ppermute | solution.py:236
  59.3 13.8 %collective-permute-start.15 = (f32[128,1024]{1,0:T(8,128)S(1)}, f32[128,1024]{1,0:T(8,128)S(1)}, u32[]{:S(2)}, u32[]{:S(2)}) collective-permute-start(f32[128,1024]{1,0:T(8,128)S(1)} %get-tuple-element.96), channel_id=1, source_target_pairs={{0,32},{16,112},{32,0},{48,80},{64,96},{80,48},{96,64},{112,16},{1... | collective-permute-start | bytes 1572872 | tf_op jit(solution)/shard_map/ppermute | solution.py:236
  66.0 11.5 %collective-permute-start.16 = (f32[64,1024]{1,0:T(8,128)S(1)}, f32[64,1024]{1,0:T(8,128)S(1)}, u32[]{:S(2)}, u32[]{:S(2)}) collective-permute-start(f32[64,1024]{1,0:T(8,128)S(1)} %get-tuple-element.102), channel_id=1, source_target_pairs={{0,96},{16,48},{32,64},{48,16},{64,32},{80,112},{96,0},{112,80},{1... | collective-permute-start | bytes 786440 | tf_op jit(solution)/shard_map/ppermute | solution.py:236
  73.3 10.2 %collective-permute-start.17 = (f32[64,1024]{1,0:T(8,128)S(1)}, f32[64,1024]{1,0:T(8,128)S(1)}, u32[]{:S(2)}, u32[]{:S(2)}) collective-permute-start(f32[64,1024]{1,0:T(8,128)S(1)} %get-tuple-element.100), channel_id=1, source_target_pairs={{0,96},{16,48},{32,64},{48,16},{64,32},{80,112},{96,0},{112,80},{1... | collective-permute-start | bytes 786440 | tf_op jit(solution)/shard_map/ppermute | solution.py:236
  77.5 9.1 %collective-permute-start.18 = (f32[64,1024]{1,0:T(8,128)S(1)}, f32[64,1024]{1,0:T(8,128)S(1)}, u32[]{:S(2)}, u32[]{:S(2)}) collective-permute-start(f32[64,1024]{1,0:T(8,128)S(1)} %add.51), channel_id=1, source_target_pairs={{0,96},{16,48},{32,64},{48,16},{64,32},{80,112},{96,0},{112,80},{1... | collective-permute-start | bytes 786440 | tf_op jit(solution)/shard_map/ppermute | solution.py:236
  83.5 5.3 %collective-permute-start.19 = (f32[64,1024]{1,0:T(8,128)S(1)}, f32[64,1024]{1,0:T(8,128)S(1)}, u32[]{:S(2)}, u32[]{:S(2)}) collective-permute-start(f32[64,1024]{1,0:T(8,128)S(1)} %add.50), channel_id=1, source_target_pairs={{0,96},{16,48},{32,64},{48,16},{64,32},{80,112},{96,0},{112,80},{1... | collective-permute-start | bytes 786440 | tf_op jit(solution)/shard_map/ppermute | solution.py:236
  88.9 9.6 %collective-permute-start.20 = (f32[128,1024]{1,0:T(8,128)S(1)}, f32[128,1024]{1,0:T(8,128)S(1)}, u32[]{:S(2)}, u32[]{:S(2)}) collective-permute-start(f32[128,1024]{1,0:T(8,128)S(1)} %constant_dynamic-update-slice_fusion.refs_0_), channel_id=1, source_target_pairs={{0,32},{16,112},{32,0},{48,80},{64,96},{80,48},{96,64},{112,16},{1... | collective-permute-start | bytes 1572872 | tf_op jit(solution)/shard_map/ppermute | solution.py:236
  91.5 14.2 %collective-permute-start.21 = (f32[128,1024]{1,0:T(8,128)S(1)}, f32[128,1024]{1,0:T(8,128)S(1)}, u32[]{:S(2)}, u32[]{:S(2)}) collective-permute-start(f32[128,1024]{1,0:T(8,128)S(1)} %constant_dynamic-update-slice_fusion.refs_0_), channel_id=1, source_target_pairs={{0,16},{16,0},{32,48},{48,32},{64,80},{80,64},{96,112},{112,96},{1... | collective-permute-start | bytes 1572872 | tf_op jit(solution)/shard_map/ppermute | solution.py:236
  98.5 7.2 %collective-permute-start.22 = (f32[128,1024]{1,0:T(8,128)S(1)}, f32[128,1024]{1,0:T(8,128)S(1)}, u32[]{:S(2)}, u32[]{:S(2)}) collective-permute-start(f32[128,1024]{1,0:T(8,128)S(1)} %collective-permute-done.20.refs_1_), channel_id=1, source_target_pairs={{0,16},{16,0},{32,48},{48,32},{64,80},{80,64},{96,112},{112,96},{1... | collective-permute-start | bytes 1572872 | tf_op jit(solution)/shard_map/ppermute | solution.py:236
  103.1 10.1 %collective-permute-start.23 = (f32[128,1024]{1,0:T(8,128)S(1)}, f32[128,1024]{1,0:T(8,128)S(1)}, u32[]{:S(2)}, u32[]{:S(2)}) collective-permute-start(f32[128,1024]{1,0:T(8,128)S(1)} %pad_maximum_fusion.2.refs_0_), channel_id=1, source_target_pairs={{0,32},{16,112},{32,0},{48,80},{64,96},{80,48},{96,64},{112,16},{1... | collective-permute-start | bytes 1572872 | tf_op jit(solution)/shard_map/ppermute | solution.py:236
  105.6 8.1 %collective-permute-start.24 = (f32[128,1024]{1,0:T(8,128)S(1)}, f32[128,1024]{1,0:T(8,128)S(1)}, u32[]{:S(2)}, u32[]{:S(2)}) collective-permute-start(f32[128,1024]{1,0:T(8,128)S(1)} %pad_maximum_fusion.2.refs_0_), channel_id=1, source_target_pairs={{0,16},{16,0},{32,48},{48,32},{64,80},{80,64},{96,112},{112,96},{1... | collective-permute-start | bytes 1572872 | tf_op jit(solution)/shard_map/ppermute | solution.py:236
  113.2 2.1 %collective-permute-start.25 = (f32[128,1024]{1,0:T(8,128)S(1)}, f32[128,1024]{1,0:T(8,128)S(1)}, u32[]{:S(2)}, u32[]{:S(2)}) collective-permute-start(f32[128,1024]{1,0:T(8,128)S(1)} %collective-permute-done.23.refs_1_), channel_id=1, source_target_pairs={{0,16},{16,0},{32,48},{48,32},{64,80},{80,64},{96,112},{112,96},{1... | collective-permute-start | bytes 1572872 | tf_op jit(solution)/shard_map/ppermute | solution.py:236

commit v3 on v2

--- a/solution.py
+++ b/solution.py
@@ -419,10 +419,10 @@
         came[c], keeps[c], factors[-1] = lax.optimization_barrier((came[c], keeps[c], factors[-1]))
         own.append(keeps[c] + came[c])
         came[c] = swap(own[c], ROW[1])
-    r_factor, ihi, ilo, bhi, blo = prepare(factors, after(rows, own[1]))
-    own, came, ihi = lax.optimization_barrier((own, came, ihi))
     own = [jnp.concatenate(p, axis=0) for p in zip(own, came)]
+    r_factor, ihi, ilo, bhi, blo = prepare(factors, after(rows, own[0]))
     came = [swap(own[0], ROW[0])]
+    came[0], ihi = lax.optimization_barrier((came[0], ihi))
     own[1] = after(own[1], came[0])
     came.append(swap(own[1], ROW[0]))
     own_across = [swap(p, CORE) for p in own]

time: 123 us -> 118 us (0.959)
  starting transfers between devices: 47.4 us -> 43.3 us
    ppermute x18, starting transfers between devices: 32.7 us -> 28.6 us  [swap(): return lax.ppermute(a, 'row', pairs)]
  transfers between devices with their start and end apart: 26 -> 26, of which waited for: 12 -> 12; matrix products, arithmetic and copies ran while one was open for 1% -> 1% of each run, Pallas kernels for 29% -> 30%
where the time goes in v3:
time: 118 us
  Pallas kernels  47.1 us (40%)
  starting transfers between devices  43.3 us (37%)
  waiting for transfers between devices  24.7 us (21%)
    ppermute x18, starting transfers between devices, swap(): return lax.ppermute(a, 'row', pairs)  28.6 us
    pallas_call x4, Pallas kernels, factor_rows(): pl.pallas_call(functools.partial(factor_kernel, k, nb), out_shape=jax.Sha...  16 us
    pallas_call x2, Pallas kernels, finish(): pl.pallas_call(functools.partial(finish_kernel, first), out_shape=(jax.Sh...  15.1 us
    ppermute x8, starting transfers between devices, gather_panel(): lax.ppermute(h, ('row', 'col'), gather_pairs(q, step))  14.7 us
    ppermute x18, waiting for transfers between devices, swap(): return lax.ppermute(a, 'row', pairs)  12.4 us
    ppermute x8, waiting for transfers between devices, gather_panel(): lax.ppermute(h, ('row', 'col'), gather_pairs(q, step))  12.3 us
    pallas_call x2, Pallas kernels, share(): pl.pallas_call(functools.partial(share_kernel, first), out_shape=(half, h...  9.04 us
    pallas_call x1, Pallas kernels, gram_share(): pl.pallas_call(gram_kernel, out_shape=(half, half), in_specs=whole(), out...  3.1 us
  transfers between devices with their start and end apart: 26, of which 12 were waited for; matrix products, arithmetic and copies ran while one was open for 1% of the time, Pallas kernels for 30%

profile of v3, /device:TPU:1, one launch (start us, length us, event | category | flops | bytes accessed | tf_op | source)
XLA Modules:
  0.0 117.9 jit_solution(616420886373203259)
XLA Ops:
  0.6 0.9 fusion
  1.5 2.2 %collective-permute-start = (f32[64,256]{1,0:T(8,128)S(1)}, f32[64,256]{1,0:T(8,128)S(1)}, u32[]{:S(2)}, u32[]{:S(2)}) collective-permute-start(f32[64,256]{1,0:T(8,128)S(1)} %get-tuple-element.98), channel_id=1, source_target_pairs={{0,1},{1,0},{2,3},{3,2},{4,5},{5,4},{6,7},{7,6},{8,9},{9,8},{10,11... | collective-permute-start | bytes 196616 | tf_op jit(solution)/shard_map/ppermute | solution.py:179
  3.7 1.9 %collective-permute-start.4 = (f32[64,256]{1,0:T(8,128)S(1)}, f32[64,256]{1,0:T(8,128)S(1)}, u32[]{:S(2)}, u32[]{:S(2)}) collective-permute-start(f32[64,256]{1,0:T(8,128)S(1)} %get-tuple-element.97), channel_id=1, source_target_pairs={{0,3},{1,2},{2,1},{3,0},{4,7},{5,6},{6,5},{7,4},{8,11},{9,10},{10,... | collective-permute-start | bytes 196616 | tf_op jit(solution)/shard_map/ppermute | solution.py:179
  5.6 2.7 %collective-permute-start.1 = (f32[128,256]{1,0:T(8,128)S(1)}, f32[128,256]{1,0:T(8,128)S(1)}, u32[]{:S(2)}, u32[]{:S(2)}) collective-permute-start(f32[128,256]{1,0:T(8,128)S(1)} %pad_maximum_fusion.6), channel_id=1, source_target_pairs={{0,3},{1,2},{2,1},{3,0},{4,7},{5,6},{6,5},{7,4},{8,11},{9,10},{10,... | collective-permute-start | bytes 393224 | tf_op jit(solution)/shard_map/ppermute | solution.py:179
  8.4 0.1 collective-permute-start.5
  8.5 2.3 %collective-permute-done.1 = f32[128,256]{1,0:T(8,128)S(1)} collective-permute-done((f32[128,256]{1,0:T(8,128)S(1)}, f32[128,256]{1,0:T(8,128)S(1)}, u32[]{:S(2)}, u32[]{:S(2)}) %collective-permute-start.1) | collective-permute-done | bytes 131104 | tf_op jit(solution)/shard_map/ppermute | solution.py:179
  10.8 1.7 %collective-permute-start.2 = (f32[256,256]{1,0:T(8,128)S(1)}, f32[256,256]{1,0:T(8,128)S(1)}, u32[]{:S(2)}, u32[]{:S(2)}) collective-permute-start(f32[256,256]{1,0:T(8,128)S(1)} %pad_maximum_fusion.4), channel_id=1, source_target_pairs={{0,4},{1,5},{2,6},{3,7},{4,0},{5,1},{6,2},{7,3},{8,12},{9,13},{10,... | collective-permute-start | bytes 786440 | tf_op jit(solution)/shard_map/ppermute | solution.py:179
  12.5 3.9 %collective-permute-start.6 = (f32[256,256]{1,0:T(8,128)S(1)}, f32[256,256]{1,0:T(8,128)S(1)}, u32[]{:S(2)}, u32[]{:S(2)}) collective-permute-start(f32[256,256]{1,0:T(8,128)S(1)} %pad_maximum_fusion.5), channel_id=1, source_target_pairs={{0,12},{1,13},{2,14},{3,15},{4,8},{5,9},{6,10},{7,11},{8,4},{9,5},... | collective-permute-start | bytes 786440 | tf_op jit(solution)/shard_map/ppermute | solution.py:179
  16.4 1.5 %collective-permute-done.2 = f32[256,256]{1,0:T(8,128)S(1)} collective-permute-done((f32[256,256]{1,0:T(8,128)S(1)}, f32[256,256]{1,0:T(8,128)S(1)}, u32[]{:S(2)}, u32[]{:S(2)}) %collective-permute-start.2) | collective-permute-done | bytes 262176 | tf_op jit(solution)/shard_map/ppermute | solution.py:179
  18.0 2.0 %collective-permute-start.3 = (f32[512,256]{1,0:T(8,128)S(1)}, f32[512,256]{1,0:T(8,128)S(1)}, u32[]{:S(2)}, u32[]{:S(2)}) collective-permute-start(f32[512,256]{1,0:T(8,128)S(1)} %pad_maximum_fusion.refs_0_), channel_id=1, source_target_pairs={{0,12},{1,13},{2,14},{3,15},{4,8},{5,9},{6,10},{7,11},{8,4},{9,5},... | collective-permute-start | bytes 1572872 | tf_op jit(solution)/shard_map/ppermute | solution.py:179
  20.0 0.2 collective-permute-done.6
  20.2 0.1 collective-permute-start.7
  20.3 7.3 %collective-permute-done.3.refs_1_ = f32[512,256]{1,0:T(8,128)S(1)} collective-permute-done((f32[512,256]{1,0:T(8,128)S(1)}, f32[512,256]{1,0:T(8,128)S(1)}, u32[]{:S(2)}, u32[]{:S(2)}) %collective-permute-start.3) | collective-permute-done | bytes 524320 | tf_op jit(solution)/shard_map/ppermute | solution.py:179
  27.6 1.0 collective-permute-done.7.refs_3_
  28.6 0.9 turn.1
  29.6 3.1 %gram.1 = (f32[640,128]{1,0:T(8,128)S(1)}, f32[640,128]{1,0:T(8,128)S(1)}) custom-call(f32[1024,512]{1,0:T(8,128)S(1)} %get-tuple-element.71.p_ref), custom_call_target="tpu_custom_call" | custom-call | flops 3000000000 | bytes 10000000 | tf_op jit(solution)/shard_map/gram/pallas_call | solution.py:223
  32.7 6.4 %collective-permute-start.8 = (f32[640,128]{1,0:T(8,128)S(1)}, f32[640,128]{1,0:T(8,128)S(1)}, u32[]{:S(2)}, u32[]{:S(2)}) collective-permute-start(f32[640,128]{1,0:T(8,128)S(1)} %get-tuple-element.49), channel_id=1, source_target_pairs={{0,16},{16,0},{32,48},{48,32},{64,80},{80,64},{96,112},{112,96},{1... | collective-permute-start | bytes 983048 | tf_op jit(solution)/shard_map/ppermute | solution.py:236
  39.1 1.3 %collective-permute-done.8 = f32[640,128]{1,0:T(8,128)S(1)} collective-permute-done((f32[640,128]{1,0:T(8,128)S(1)}, f32[640,128]{1,0:T(8,128)S(1)}, u32[]{:S(2)}, u32[]{:S(2)}) %collective-permute-start.8) | collective-permute-done | bytes 327712 | tf_op jit(solution)/shard_map/ppermute | solution.py:236
  40.4 2.6 %collective-permute-start.11 = (f32[640,128]{1,0:T(8,128)S(1)}, f32[640,128]{1,0:T(8,128)S(1)}, u32[]{:S(2)}, u32[]{:S(2)}) collective-permute-start(f32[640,128]{1,0:T(8,128)S(1)} %add.39), channel_id=1, source_target_pairs={{0,32},{16,112},{32,0},{48,80},{64,96},{80,48},{96,64},{112,16},{1... | collective-permute-start | bytes 983048 | tf_op jit(solution)/shard_map/ppermute | solution.py:236
  42.9 4.5 %share.2 = (f32[256,1024]{1,0:T(8,128)S(1)}, f32[256,1024]{1,0:T(8,128)S(1)}) custom-call(bf16[512,1024]{1,0:T(8,128)(2,1)S(1)} %get-tuple-element.55.hi_ref, bf16[512,1024]{1,0:T(8,128)(2,1)S(1)} %get-tuple-element.51.lo_ref, f32[1024,2048]{1,0:T(8,128)S(1)} %bitcast.1), custom_call_target="tpu_custom_call" | custom-call | flops 3000000000 | bytes 10000000 | tf_op jit(solution)/shard_map/share/pallas_call | solution.py:269
  47.5 0.1 collective-permute-start.9
  47.6 0.4 collective-permute-start.12
  48.0 4.5 %share.3 = (f32[256,1024]{1,0:T(8,128)S(1)}, f32[256,1024]{1,0:T(8,128)S(1)}) custom-call(bf16[512,1024]{1,0:T(8,128)(2,1)S(1)} %get-tuple-element.55.hi_ref, bf16[512,1024]{1,0:T(8,128)(2,1)S(1)} %get-tuple-element.51.lo_ref, f32[1024,2048]{1,0:T(8,128)S(1)} %bitcast.1), custom_call_target="tpu_custom_call" | custom-call | flops 3000000000 | bytes 10000000 | tf_op jit(solution)/shard_map/share/pallas_call | solution.py:269
  52.5 1.4 %collective-permute-done.12 = f32[640,128]{1,0:T(8,128)S(1)} collective-permute-done((f32[640,128]{1,0:T(8,128)S(1)}, f32[640,128]{1,0:T(8,128)S(1)}, u32[]{:S(2)}, u32[]{:S(2)}) %collective-permute-start.12) | collective-permute-done | bytes 327712 | tf_op jit(solution)/shard_map/ppermute | solution.py:236
  53.9 2.6 %collective-permute-start.14 = (f32[256,1024]{1,0:T(8,128)S(1)}, f32[256,1024]{1,0:T(8,128)S(1)}, u32[]{:S(2)}, u32[]{:S(2)}) collective-permute-start(f32[256,1024]{1,0:T(8,128)S(1)} %get-tuple-element.61), channel_id=1, source_target_pairs={{0,16},{16,0},{32,48},{48,32},{64,80},{80,64},{96,112},{112,96},{1... | collective-permute-start | bytes 3145736 | tf_op jit(solution)/shard_map/ppermute | solution.py:236
  56.6 0.2 slice_add_fusion.2
  56.8 2.4 %collective-permute-start.10 = (f32[128,1024]{1,0:T(8,128)S(1)}, f32[128,1024]{1,0:T(8,128)S(1)}, u32[]{:S(2)}, u32[]{:S(2)}) collective-permute-start(f32[128,1024]{1,0:T(8,128)S(1)} %get-tuple-element.92), channel_id=1, source_target_pairs={{0,32},{16,112},{32,0},{48,80},{64,96},{80,48},{96,64},{112,16},{1... | collective-permute-start | bytes 1572872 | tf_op jit(solution)/shard_map/ppermute | solution.py:236
  59.2 0.2 slice_add_fusion
  59.3 2.3 %collective-permute-start.15 = (f32[128,1024]{1,0:T(8,128)S(1)}, f32[128,1024]{1,0:T(8,128)S(1)}, u32[]{:S(2)}, u32[]{:S(2)}) collective-permute-start(f32[128,1024]{1,0:T(8,128)S(1)} %get-tuple-element.90), channel_id=1, source_target_pairs={{0,32},{16,112},{32,0},{48,80},{64,96},{80,48},{96,64},{112,16},{1... | collective-permute-start | bytes 1572872 | tf_op jit(solution)/shard_map/ppermute | solution.py:236
  61.6 3.6 %factor.4.refs_0_.w0 = f32[128,640]{1,0:T(8,128)S(1)} custom-call(f32[640,128]{1,0:T(8,128)S(1)} %add.43.refs_0_.refs_1_.refs_2_.refs_3_, f32[640,128]{1,0:T(8,128)S(1)} %collective-permute-done.13.refs_1_.refs_2_.refs_3_.refs_4_), custom_call_target="tpu_custom_call" | custom-call | flops 300000000 | bytes 1000000 | tf_op jit(solution)/shard_map/factor/pallas_call | solution.py:150
  65.3 0.8 collective-permute-done.10
  66.1 0.1 collective-permute-start.16
  66.2 4.0 %factor.5.refs_1_.w1 = f32[128,640]{1,0:T(8,128)S(1)} custom-call(f32[128,640]{1,0:T(8,128)S(1)} %factor.4.refs_0_.w0, f32[640,128]{1,0:T(8,128)S(1)} %add.43.refs_0_.refs_1_.refs_2_.refs_3_, f32[640,128]{1,0:T(8,128)S(1)} %collective-permute-done.13.refs_1_.refs_2_.refs_3_.refs_4_), custom_call_target="tpu_custom_call" | custom-call | flops 300000000 | bytes 1000000 | tf_op jit(solution)/shard_map/factor/pallas_call | solution.py:150
  70.3 3.1 %collective-permute-done.15 = f32[128,1024]{1,0:T(8,128)S(1)} collective-permute-done((f32[128,1024]{1,0:T(8,128)S(1)}, f32[128,1024]{1,0:T(8,128)S(1)}, u32[]{:S(2)}, u32[]{:S(2)}) %collective-permute-start.15) | collective-permute-done | bytes 524320 | tf_op jit(solution)/shard_map/ppermute | solution.py:236
  73.3 4.1 %factor.6.refs_2_.w2 = f32[128,640]{1,0:T(8,128)S(1)} custom-call(f32[128,640]{1,0:T(8,128)S(1)} %factor.4.refs_0_.w0, f32[128,640]{1,0:T(8,128)S(1)} %factor.5.refs_1_.w1, f32[640,128]{1,0:T(8,128)S(1)} %add.43.refs_0_.refs_1_.refs_2_.refs_3_, f32[640,128]{1,0:T(8,128)S(1)} %collective-permute-done.13.refs_1_.refs_2_.refs_3_.refs_4_), custom_call_target="tpu_custom_call" | custom-call | flops 300000000 | bytes 1000000 | tf_op jit(solution)/shard_map/factor/pallas_call | solution.py:150
  77.7 1.5 %collective-permute-start.17 = (f32[64,1024]{1,0:T(8,128)S(1)}, f32[64,1024]{1,0:T(8,128)S(1)}, u32[]{:S(2)}, u32[]{:S(2)}) collective-permute-start(f32[64,1024]{1,0:T(8,128)S(1)} %get-tuple-element.94), channel_id=1, source_target_pairs={{0,96},{16,48},{32,64},{48,16},{64,32},{80,112},{96,0},{112,80},{1... | collective-permute-start | bytes 786440 | tf_op jit(solution)/shard_map/ppermute | solution.py:236
  79.2 3.9 %collective-permute-done.18 = f32[64,1024]{1,0:T(8,128)S(1)} collective-permute-done((f32[64,1024]{1,0:T(8,128)S(1)}, f32[64,1024]{1,0:T(8,128)S(1)}, u32[]{:S(2)}, u32[]{:S(2)}) %collective-permute-start.18) | collective-permute-done | bytes 262176 | tf_op jit(solution)/shard_map/ppermute | solution.py:236
  83.2 2.6 %collective-permute-start.20 = (f32[128,1024]{1,0:T(8,128)S(1)}, f32[128,1024]{1,0:T(8,128)S(1)}, u32[]{:S(2)}, u32[]{:S(2)}) collective-permute-start(f32[128,1024]{1,0:T(8,128)S(1)} %pad_maximum_fusion.2.refs_0_), channel_id=1, source_target_pairs={{0,32},{16,112},{32,0},{48,80},{64,96},{80,48},{96,64},{112,16},{1... | collective-permute-start | bytes 1572872 | tf_op jit(solution)/shard_map/ppermute | solution.py:236
  85.8 4.2 %factor.7.w3 = f32[128,640]{1,0:T(8,128)S(1)} custom-call(f32[128,640]{1,0:T(8,128)S(1)} %factor.4.refs_0_.w0, f32[128,640]{1,0:T(8,128)S(1)} %factor.5.refs_1_.w1, f32[128,640]{1,0:T(8,128)S(1)} %factor.6.refs_2_.w2, f32[640,128]{1,0:T(8,128)S(1)} %add.43.refs_0_.refs_1_.refs_2_.refs_3_, f32[640,128]{1,0:T(8,128)S(1)} %collective-permute-done.13.refs_1_.refs_2_.refs_3_.refs_4_), custom_call_target="tpu_custom_call" | custom-call | flops 300000000 | bytes 1000000 | tf_op jit(solution)/shard_map/factor/pallas_call | solution.py:150
  90.1 2.9 %collective-permute-start.21 = (f32[128,1024]{1,0:T(8,128)S(1)}, f32[128,1024]{1,0:T(8,128)S(1)}, u32[]{:S(2)}, u32[]{:S(2)}) collective-permute-start(f32[128,1024]{1,0:T(8,128)S(1)} %pad_maximum_fusion.2.refs_0_), channel_id=1, source_target_pairs={{0,16},{16,0},{32,48},{48,32},{64,80},{80,64},{96,112},{112,96},{1... | collective-permute-start | bytes 1572872 | tf_op jit(solution)/shard_map/ppermute | solution.py:236
  93.1 3.0 %prepare.1 = (f32[512,512]{1,0:T(8,128)}, bf16[512,512]{1,0:T(8,128)(2,1)S(1)}, bf16[512,512]{1,0:T(8,128)(2,1)S(1)}, bf16[1024,512]{1,0:T(8,128)(2,1)S(1)}, bf16[1024,512]{1,0:T(8,128)(2,1)S(1)}) custom-call(f32[128,640]{1,0:T(8,128)S(1)} %factor.4.refs_0_.w0, f32[128,640]{1,0:T(8,128)S(1)} %factor.5.refs_1_.w1, f32[128,640]{1,0:T(8,128)S(1)} %factor.6.refs_2_.w2, ...), custom_call_target="tpu_custom_call" | custom-call | flops 300000000 | bytes 1000000 | tf_op jit(solution)/shard_map/prepare/pallas_call | solution.py:309
  96.1 1.2 %collective-permute-start.22 = (f32[128,1024]{1,0:T(8,128)S(1)}, f32[128,1024]{1,0:T(8,128)S(1)}, u32[]{:S(2)}, u32[]{:S(2)}) collective-permute-start(f32[128,1024]{1,0:T(8,128)S(1)} %collective-permute-done.20.refs_1_), channel_id=1, source_target_pairs={{0,16},{16,0},{32,48},{48,32},{64,80},{80,64},{96,112},{112,96},{1... | collective-permute-start | bytes 1572872 | tf_op jit(solution)/shard_map/ppermute | solution.py:236
  97.3 0.4 collective-permute-done.19
  97.7 2.8 %collective-permute-start.23 = (f32[128,1024]{1,0:T(8,128)S(1)}, f32[128,1024]{1,0:T(8,128)S(1)}, u32[]{:S(2)}, u32[]{:S(2)}) collective-permute-start(f32[128,1024]{1,0:T(8,128)S(1)} %pad_maximum_fusion.3.refs_0_), channel_id=1, source_target_pairs={{0,32},{16,112},{32,0},{48,80},{64,96},{80,48},{96,64},{112,16},{1... | collective-permute-start | bytes 1572872 | tf_op jit(solution)/shard_map/ppermute | solution.py:236
  100.5 7.5 %finish.2 = (f32[512,2048]{1,0:T(8,128)}, f32[1024,2048]{1,0:T(8,128)}) custom-call(f32[128,1024]{1,0:T(8,128)S(1)} %pad_maximum_fusion.2.refs_0_, f32[128,1024]{1,0:T(8,128)S(1)} %collective-permute-done.20.refs_1_, f32[128,1024]{1,0:T(8,128)S(1)} %collective-permute-done.21.refs_2_, f32[128,1024]{1,0:T(8,128)S(1)} %collective-permute-done.22.refs_3_, ...), custom_call_target="tpu_custom_call" | custom-call | flops 300000000 | bytes 1000000 | tf_op jit(solution)/shard_map/finish/pallas_call | solution.py:365
  108.1 0.6 collective-permute-start.25
  108.7 1.5 %collective-permute-done.25.refs_3_ = f32[128,1024]{1,0:T(8,128)S(1)} collective-permute-done((f32[128,1024]{1,0:T(8,128)S(1)}, f32[128,1024]{1,0:T(8,128)S(1)}, u32[]{:S(2)}, u32[]{:S(2)}) %collective-permute-start.25) | collective-permute-done | bytes 524320 | tf_op jit(solution)/shard_map/ppermute | solution.py:236
  110.2 7.5 %finish.3 = (f32[512,2048]{1,0:T(8,128)}, f32[1024,2048]{1,0:T(8,128)}) custom-call(f32[128,1024]{1,0:T(8,128)S(1)} %pad_maximum_fusion.3.refs_0_, f32[128,1024]{1,0:T(8,128)S(1)} %collective-permute-done.23.refs_1_, f32[128,1024]{1,0:T(8,128)S(1)} %collective-permute-done.24.refs_2_, ...), custom_call_target="tpu_custom_call", output_to_operand_aliasing={{0}: (9, {}), {1}: (10, {})} | custom-call | flops 300000000 | bytes 1000000 | tf_op jit(solution)/shard_map/finish/pallas_call | solution.py:365
  (38 shorter events, 0.7 us)
Async XLA Ops:
  1.5 4.1 %collective-permute-start = (f32[64,256]{1,0:T(8,128)S(1)}, f32[64,256]{1,0:T(8,128)S(1)}, u32[]{:S(2)}, u32[]{:S(2)}) collective-permute-start(f32[64,256]{1,0:T(8,128)S(1)} %get-tuple-element.98), channel_id=1, source_target_pairs={{0,1},{1,0},{2,3},{3,2},{4,5},{5,4},{6,7},{7,6},{8,9},{9,8},{10,11... | collective-permute-start | bytes 196616 | tf_op jit(solution)/shard_map/ppermute | solution.py:179
  3.7 4.7 %collective-permute-start.4 = (f32[64,256]{1,0:T(8,128)S(1)}, f32[64,256]{1,0:T(8,128)S(1)}, u32[]{:S(2)}, u32[]{:S(2)}) collective-permute-start(f32[64,256]{1,0:T(8,128)S(1)} %get-tuple-element.97), channel_id=1, source_target_pairs={{0,3},{1,2},{2,1},{3,0},{4,7},{5,6},{6,5},{7,4},{8,11},{9,10},{10,... | collective-permute-start | bytes 196616 | tf_op jit(solution)/shard_map/ppermute | solution.py:179
  5.6 5.1 %collective-permute-start.1 = (f32[128,256]{1,0:T(8,128)S(1)}, f32[128,256]{1,0:T(8,128)S(1)}, u32[]{:S(2)}, u32[]{:S(2)}) collective-permute-start(f32[128,256]{1,0:T(8,128)S(1)} %pad_maximum_fusion.6), channel_id=1, source_target_pairs={{0,3},{1,2},{2,1},{3,0},{4,7},{5,6},{6,5},{7,4},{8,11},{9,10},{10,... | collective-permute-start | bytes 393224 | tf_op jit(solution)/shard_map/ppermute | solution.py:179
  8.4 4.1 %collective-permute-start.5 = (f32[128,256]{1,0:T(8,128)S(1)}, f32[128,256]{1,0:T(8,128)S(1)}, u32[]{:S(2)}, u32[]{:S(2)}) collective-permute-start(f32[128,256]{1,0:T(8,128)S(1)} %pad_maximum_fusion.7), channel_id=1, source_target_pairs={{0,1},{1,0},{2,3},{3,2},{4,5},{5,4},{6,7},{7,6},{8,9},{9,8},{10,11... | collective-permute-start | bytes 393224 | tf_op jit(solution)/shard_map/ppermute | solution.py:179
  10.8 7.2 %collective-permute-start.2 = (f32[256,256]{1,0:T(8,128)S(1)}, f32[256,256]{1,0:T(8,128)S(1)}, u32[]{:S(2)}, u32[]{:S(2)}) collective-permute-start(f32[256,256]{1,0:T(8,128)S(1)} %pad_maximum_fusion.4), channel_id=1, source_target_pairs={{0,4},{1,5},{2,6},{3,7},{4,0},{5,1},{6,2},{7,3},{8,12},{9,13},{10,... | collective-permute-start | bytes 786440 | tf_op jit(solution)/shard_map/ppermute | solution.py:179
  12.5 7.7 %collective-permute-start.6 = (f32[256,256]{1,0:T(8,128)S(1)}, f32[256,256]{1,0:T(8,128)S(1)}, u32[]{:S(2)}, u32[]{:S(2)}) collective-permute-start(f32[256,256]{1,0:T(8,128)S(1)} %pad_maximum_fusion.5), channel_id=1, source_target_pairs={{0,12},{1,13},{2,14},{3,15},{4,8},{5,9},{6,10},{7,11},{8,4},{9,5},... | collective-permute-start | bytes 786440 | tf_op jit(solution)/shard_map/ppermute | solution.py:179
  18.0 9.6 %collective-permute-start.3 = (f32[512,256]{1,0:T(8,128)S(1)}, f32[512,256]{1,0:T(8,128)S(1)}, u32[]{:S(2)}, u32[]{:S(2)}) collective-permute-start(f32[512,256]{1,0:T(8,128)S(1)} %pad_maximum_fusion.refs_0_), channel_id=1, source_target_pairs={{0,12},{1,13},{2,14},{3,15},{4,8},{5,9},{6,10},{7,11},{8,4},{9,5},... | collective-permute-start | bytes 1572872 | tf_op jit(solution)/shard_map/ppermute | solution.py:179
  20.2 8.4 %collective-permute-start.7 = (f32[512,256]{1,0:T(8,128)S(1)}, f32[512,256]{1,0:T(8,128)S(1)}, u32[]{:S(2)}, u32[]{:S(2)}) collective-permute-start(f32[512,256]{1,0:T(8,128)S(1)} %pad_maximum_fusion.1.refs_2_), channel_id=1, source_target_pairs={{0,4},{1,5},{2,6},{3,7},{4,0},{5,1},{6,2},{7,3},{8,12},{9,13},{10,... | collective-permute-start | bytes 1572872 | tf_op jit(solution)/shard_map/ppermute | solution.py:179
  28.6 14.3 %slice-start = ((s8[8388608]{0:T(1024)(128)(4,1)}), s8[4194304]{0:T(1024)(128)(4,1)S(1)}, s32[]{:S(2)}) async-start(s8[8388608]{0:T(1024)(128)(4,1)} %bitcast), calls=%async_computation | async-start | bytes 8388608
  29.6 13.4 %slice-start.1 = ((s8[8388608]{0:T(1024)(128)(4,1)}), s8[4194304]{0:T(1024)(128)(4,1)S(1)}, s32[]{:S(2)}) async-start(s8[8388608]{0:T(1024)(128)(4,1)} %bitcast), calls=%async_computation.1 | async-start | bytes 8388608
  32.7 7.6 %collective-permute-start.8 = (f32[640,128]{1,0:T(8,128)S(1)}, f32[640,128]{1,0:T(8,128)S(1)}, u32[]{:S(2)}, u32[]{:S(2)}) collective-permute-start(f32[640,128]{1,0:T(8,128)S(1)} %get-tuple-element.49), channel_id=1, source_target_pairs={{0,16},{16,0},{32,48},{48,32},{64,80},{80,64},{96,112},{112,96},{1... | collective-permute-start | bytes 983048 | tf_op jit(solution)/shard_map/ppermute | solution.py:236
  40.4 7.2 %collective-permute-start.11 = (f32[640,128]{1,0:T(8,128)S(1)}, f32[640,128]{1,0:T(8,128)S(1)}, u32[]{:S(2)}, u32[]{:S(2)}) collective-permute-start(f32[640,128]{1,0:T(8,128)S(1)} %add.39), channel_id=1, source_target_pairs={{0,32},{16,112},{32,0},{48,80},{64,96},{80,48},{96,64},{112,16},{1... | collective-permute-start | bytes 983048 | tf_op jit(solution)/shard_map/ppermute | solution.py:236
  47.5 9.1 %collective-permute-start.9 = (f32[256,1024]{1,0:T(8,128)S(1)}, f32[256,1024]{1,0:T(8,128)S(1)}, u32[]{:S(2)}, u32[]{:S(2)}) collective-permute-start(f32[256,1024]{1,0:T(8,128)S(1)} %get-tuple-element.53), channel_id=1, source_target_pairs={{0,16},{16,0},{32,48},{48,32},{64,80},{80,64},{96,112},{112,96},{1... | collective-permute-start | bytes 3145736 | tf_op jit(solution)/shard_map/ppermute | solution.py:236
  47.6 6.3 %collective-permute-start.12 = (f32[640,128]{1,0:T(8,128)S(1)}, f32[640,128]{1,0:T(8,128)S(1)}, u32[]{:S(2)}, u32[]{:S(2)}) collective-permute-start(f32[640,128]{1,0:T(8,128)S(1)} %add.42), channel_id=1, source_target_pairs={{0,96},{16,48},{32,64},{48,16},{64,32},{80,112},{96,0},{112,80},{1... | collective-permute-start | bytes 983048 | tf_op jit(solution)/shard_map/ppermute | solution.py:236
  53.9 5.2 %collective-permute-start.14 = (f32[256,1024]{1,0:T(8,128)S(1)}, f32[256,1024]{1,0:T(8,128)S(1)}, u32[]{:S(2)}, u32[]{:S(2)}) collective-permute-start(f32[256,1024]{1,0:T(8,128)S(1)} %get-tuple-element.61), channel_id=1, source_target_pairs={{0,16},{16,0},{32,48},{48,32},{64,80},{80,64},{96,112},{112,96},{1... | collective-permute-start | bytes 3145736 | tf_op jit(solution)/shard_map/ppermute | solution.py:236
  56.8 9.3 %collective-permute-start.10 = (f32[128,1024]{1,0:T(8,128)S(1)}, f32[128,1024]{1,0:T(8,128)S(1)}, u32[]{:S(2)}, u32[]{:S(2)}) collective-permute-start(f32[128,1024]{1,0:T(8,128)S(1)} %get-tuple-element.92), channel_id=1, source_target_pairs={{0,32},{16,112},{32,0},{48,80},{64,96},{80,48},{96,64},{112,16},{1... | collective-permute-start | bytes 1572872 | tf_op jit(solution)/shard_map/ppermute | solution.py:236
  59.2 2.5 %collective-permute-start.13 = (f32[640,128]{1,0:T(8,128)S(1)}, f32[640,128]{1,0:T(8,128)S(1)}, u32[]{:S(2)}, u32[]{:S(2)}) collective-permute-start(f32[640,128]{1,0:T(8,128)S(1)} %add.43.refs_0_.refs_1_.refs_2_.refs_3_), channel_id=1, source_target_pairs={{0,16},{16,0},{32,48},{48,32},{64,80},{80,64},{96,112},{112,96},{1... | collective-permute-start | bytes 983048 | tf_op jit(solution)/shard_map/ppermute | solution.py:236
  59.3 14.0 %collective-permute-start.15 = (f32[128,1024]{1,0:T(8,128)S(1)}, f32[128,1024]{1,0:T(8,128)S(1)}, u32[]{:S(2)}, u32[]{:S(2)}) collective-permute-start(f32[128,1024]{1,0:T(8,128)S(1)} %get-tuple-element.90), channel_id=1, source_target_pairs={{0,32},{16,112},{32,0},{48,80},{64,96},{80,48},{96,64},{112,16},{1... | collective-permute-start | bytes 1572872 | tf_op jit(solution)/shard_map/ppermute | solution.py:236
  66.1 11.3 %collective-permute-start.16 = (f32[64,1024]{1,0:T(8,128)S(1)}, f32[64,1024]{1,0:T(8,128)S(1)}, u32[]{:S(2)}, u32[]{:S(2)}) collective-permute-start(f32[64,1024]{1,0:T(8,128)S(1)} %get-tuple-element.96), channel_id=1, source_target_pairs={{0,96},{16,48},{32,64},{48,16},{64,32},{80,112},{96,0},{112,80},{1... | collective-permute-start | bytes 786440 | tf_op jit(solution)/shard_map/ppermute | solution.py:236
  77.5 5.6 %collective-permute-start.18 = (f32[64,1024]{1,0:T(8,128)S(1)}, f32[64,1024]{1,0:T(8,128)S(1)}, u32[]{:S(2)}, u32[]{:S(2)}) collective-permute-start(f32[64,1024]{1,0:T(8,128)S(1)} %add.50), channel_id=1, source_target_pairs={{0,96},{16,48},{32,64},{48,16},{64,32},{80,112},{96,0},{112,80},{1... | collective-permute-start | bytes 786440 | tf_op jit(solution)/shard_map/ppermute | solution.py:236
  77.7 12.3 %collective-permute-start.17 = (f32[64,1024]{1,0:T(8,128)S(1)}, f32[64,1024]{1,0:T(8,128)S(1)}, u32[]{:S(2)}, u32[]{:S(2)}) collective-permute-start(f32[64,1024]{1,0:T(8,128)S(1)} %get-tuple-element.94), channel_id=1, source_target_pairs={{0,96},{16,48},{32,64},{48,16},{64,32},{80,112},{96,0},{112,80},{1... | collective-permute-start | bytes 786440 | tf_op jit(solution)/shard_map/ppermute | solution.py:236
  83.2 12.9 %collective-permute-start.20 = (f32[128,1024]{1,0:T(8,128)S(1)}, f32[128,1024]{1,0:T(8,128)S(1)}, u32[]{:S(2)}, u32[]{:S(2)}) collective-permute-start(f32[128,1024]{1,0:T(8,128)S(1)} %pad_maximum_fusion.2.refs_0_), channel_id=1, source_target_pairs={{0,32},{16,112},{32,0},{48,80},{64,96},{80,48},{96,64},{112,16},{1... | collective-permute-start | bytes 1572872 | tf_op jit(solution)/shard_map/ppermute | solution.py:236
  90.0 7.6 %collective-permute-start.19 = (f32[64,1024]{1,0:T(8,128)S(1)}, f32[64,1024]{1,0:T(8,128)S(1)}, u32[]{:S(2)}, u32[]{:S(2)}) collective-permute-start(f32[64,1024]{1,0:T(8,128)S(1)} %add.51), channel_id=1, source_target_pairs={{0,96},{16,48},{32,64},{48,16},{64,32},{80,112},{96,0},{112,80},{1... | collective-permute-start | bytes 786440 | tf_op jit(solution)/shard_map/ppermute | solution.py:236
  90.1 10.4 %collective-permute-start.21 = (f32[128,1024]{1,0:T(8,128)S(1)}, f32[128,1024]{1,0:T(8,128)S(1)}, u32[]{:S(2)}, u32[]{:S(2)}) collective-permute-start(f32[128,1024]{1,0:T(8,128)S(1)} %pad_maximum_fusion.2.refs_0_), channel_id=1, source_target_pairs={{0,16},{16,0},{32,48},{48,32},{64,80},{80,64},{96,112},{112,96},{1... | collective-permute-start | bytes 1572872 | tf_op jit(solution)/shard_map/ppermute | solution.py:236
  96.1 4.5 %collective-permute-start.22 = (f32[128,1024]{1,0:T(8,128)S(1)}, f32[128,1024]{1,0:T(8,128)S(1)}, u32[]{:S(2)}, u32[]{:S(2)}) collective-permute-start(f32[128,1024]{1,0:T(8,128)S(1)} %collective-permute-done.20.refs_1_), channel_id=1, source_target_pairs={{0,16},{16,0},{32,48},{48,32},{64,80},{80,64},{96,112},{112,96},{1... | collective-permute-start | bytes 1572872 | tf_op jit(solution)/shard_map/ppermute | solution.py:236
  97.7 10.4 %collective-permute-start.23 = (f32[128,1024]{1,0:T(8,128)S(1)}, f32[128,1024]{1,0:T(8,128)S(1)}, u32[]{:S(2)}, u32[]{:S(2)}) collective-permute-start(f32[128,1024]{1,0:T(8,128)S(1)} %pad_maximum_fusion.3.refs_0_), channel_id=1, source_target_pairs={{0,32},{16,112},{32,0},{48,80},{64,96},{80,48},{96,64},{112,16},{1... | collective-permute-start | bytes 1572872 | tf_op jit(solution)/shard_map/ppermute | solution.py:236
  100.5 8.1 %collective-permute-start.24 = (f32[128,1024]{1,0:T(8,128)S(1)}, f32[128,1024]{1,0:T(8,128)S(1)}, u32[]{:S(2)}, u32[]{:S(2)}) collective-permute-start(f32[128,1024]{1,0:T(8,128)S(1)} %pad_maximum_fusion.3.refs_0_), channel_id=1, source_target_pairs={{0,16},{16,0},{32,48},{48,32},{64,80},{80,64},{96,112},{112,96},{1... | collective-permute-start | bytes 1572872 | tf_op jit(solution)/shard_map/ppermute | solution.py:236
  108.1 2.1 %collective-permute-start.25 = (f32[128,1024]{1,0:T(8,128)S(1)}, f32[128,1024]{1,0:T(8,128)S(1)}, u32[]{:S(2)}, u32[]{:S(2)}) collective-permute-start(f32[128,1024]{1,0:T(8,128)S(1)} %collective-permute-done.23.refs_1_), channel_id=1, source_target_pairs={{0,16},{16,0},{32,48},{48,32},{64,80},{80,64},{96,112},{112,96},{1... | collective-permute-start | bytes 1572872 | tf_op jit(solution)/shard_map/ppermute | solution.py:236
